TPU v7x, 1024 devices: a whole 4x4x32 slice. The times are simulated.
1024 devices in a mesh: wide: 64 (over z_hi, x, y, core), narrow: 16 (over z_lo).
Axes of the slice: x: 4, y: 4, z: 32 (z_hi: 2, z_lo: 16; z = z_hi * 16 + z_lo), core: 2. Of those that a mesh axis runs over, the one named last changes fastest.
Arguments:
- state: bfloat16 [262144, 128], P(('wide', 'narrow')), may hold values from 0.0099487305 to 1
- block_values: bfloat16 [512, 16, 128, 128], P('wide', 'narrow'), may hold values from 0.00019454956 to 0.0078125
- block_rows: int32 [512, 16], P('wide', 'narrow'), may hold values from 0 to 31
- block_cols: int32 [512, 16], P('wide', 'narrow'), may hold values from 0 to 127
- anchor_ids: int32 [8192], P(('wide', 'narrow')), may hold values from 0 to 262143, as said below
- anchor_class: int32 [8192], P(('wide', 'narrow')), may hold values from 0 to 127
Outputs:
- labels_out: bfloat16 [262144, 128], P(('wide', 'narrow'))
Inputs may be any that keep to these rules, and one draw needn't show every extreme that they name: The 8 ids of each aligned block of anchor_ids are distinct documents among the 256 rows of that block's device, in order of devices.
All inputs are finite; a program needn't handle non-finite values.
Results may differ from a plain program's by a relative error of at most 0.0045.
Values may be sent and summed in bfloat16 or wider, within the bound.
No kernel may reach another device: no remote copies, remote signals or barrier semaphores. Data moves between devices by JAX's collectives and lax.ppermute only.
A program may use at most 32 MiB of HBM per device.

v0:
```python
import jax
import jax.numpy as jnp
from jax import lax
from jax.sharding import PartitionSpec as P


def local(state, block_values, block_rows, block_cols, anchor_ids, anchor_class):
    doc_dev, labels = state.shape
    width = block_values.shape[2]
    panel_blocks = lax.axis_size("narrow") * (doc_dev // width)
    group_blocks = lax.axis_size("wide") * (doc_dev // width)
    values = block_values[:, 0]
    cols = block_cols[:, 0]
    owners = jax.nn.one_hot(block_rows[:, 0], panel_blocks, dtype=jnp.float32)
    first_row = lax.axis_index(("wide", "narrow")) * doc_dev
    local_ids = anchor_ids - first_row
    match = (local_ids[:, None] == jnp.arange(doc_dev, dtype=jnp.int32)[None, :]).astype(
        jnp.float32
    )
    anchored = jnp.sum(match, axis=0) > 0.5
    fixed = jnp.dot(match.T, jax.nn.one_hot(anchor_class, labels, dtype=jnp.float32))
    current = state
    gathered = lax.all_gather(current, "wide", axis=0, tiled=True)
    blocks = gathered.reshape(group_blocks, width, labels)
    picked = blocks[cols]
    contrib = jnp.einsum("krm,kml->krl", values, picked, preferred_element_type=jnp.float32)
    partial_sum = jnp.einsum("kb,krl->brl", owners, contrib)
    sums = lax.psum_scatter(
        partial_sum.reshape(panel_blocks * width, labels).astype(jnp.bfloat16),
        "narrow",
        scatter_dimension=0,
        tiled=True,
    ).astype(jnp.float32)
    total = sums + current.astype(jnp.float32)
    spread = total / jnp.sum(total, axis=-1, keepdims=True)
    spread = jnp.where(anchored[:, None], fixed, spread)
    current = spread.astype(jnp.bfloat16)
    return current


def solution(mesh):
    in_specs = (
        P(("wide", "narrow"), None),
        P("wide", "narrow", None, None),
        P("wide", "narrow"),
        P("wide", "narrow"),
        P(("wide", "narrow")),
        P(("wide", "narrow")),
    )
    out_specs = P(("wide", "narrow"), None)
    return jax.shard_map(local, mesh=mesh, in_specs=in_specs, out_specs=out_specs, check_vma=False)
```

profile of v0, /device:TPU:12, one launch (start us, length us, event | category | flops | bytes accessed | tf_op | source)
XLA Modules:
  0.0 431.6 jit_solution(600629549463658823)
XLA Ops:
  6.5 0.0 copy-start
  6.5 0.0 copy-start.1
  6.5 0.0 copy-start.2
  6.5 0.0 copy-start.3
  6.5 0.0 all-gather.2.cloned.1.call-start
  6.6 0.7 all-gather.2.cloned.1.call-update
  7.3 0.0 reduce-scatter.2.cloned.1.call-start
  7.3 0.7 fusion.10
  8.0 224.3 %all-gather.2.cloned.1.call-done = bf16[16384,128]{1,0:T(8,128)(2,1)} async-done(((bf16[256,128]{1,0:T(8,128)(2,1)}), bf16[16384,128]{1,0:T(8,128)(2,1)}) %all-gather.2.cloned.1.call-update) | async-done | bytes 4194320 | tf_op jit(solution)/shard_map/all_gather | solution.py:23
  232.3 2.8 gather_fusion
  235.1 0.0 copy-done
  235.1 0.3 fusion.2
  235.4 0.2 copy.9
  235.6 1.2 convolution_convert_fusion
  236.8 1.4 copy.8
  238.2 0.0 reduce-scatter.2.cloned.1.call-update
  238.2 0.0 copy-done.2
  238.3 0.1 convert_reduce_fusion
  238.4 183.7 %reduce-scatter.2.cloned.1.call-done = bf16[256,128]{1,0:T(8,128)(2,1)} async-done(((bf16[4096,128]{1,0:T(8,128)(2,1)}), bf16[256,128]{1,0:T(8,128)(2,1)}) %reduce-scatter.2.cloned.1.call-update) | async-done | bytes 65552 | tf_op jit(solution)/shard_map/reduce_scatter | solution.py:28
  422.0 0.0 copy-done.1
  422.0 1.0 fusion.4
  423.0 0.0 copy-done.3
  423.0 1.8 fusion
  (3 shorter events, 0.0 us)
Async XLA Ops:
  6.5 228.5 %copy-start = (bf16[8,1,128,128]{3,2,1,0:T(8,128)(2,1)S(1)}, bf16[8,1,128,128]{3,2,1,0:T(8,128)(2,1)}, u32[]{:S(2)}) copy-start(bf16[8,1,128,128]{3,2,1,0:T(8,128)(2,1)} %param.7) | copy-start | bytes 786436
  6.5 415.5 %copy-start.1 = (bf16[256,128]{1,0:T(8,128)(2,1)S(1)}, bf16[256,128]{1,0:T(8,128)(2,1)}, u32[]{:S(2)}) copy-start(bf16[256,128]{1,0:T(8,128)(2,1)} %param.6) | copy-start | bytes 196612
  6.5 231.7 %copy-start.2 = (s32[8]{0:T(128)S(1)}, s32[8]{0:T(128)}, u32[]{:S(2)}) copy-start(s32[8]{0:T(128)} %param.10) | copy-start | bytes 100
  6.5 416.5 %copy-start.3 = (s32[8]{0:T(128)S(1)}, s32[8]{0:T(128)}, u32[]{:S(2)}) copy-start(s32[8]{0:T(128)} %param.11) | copy-start | bytes 100
  6.5 225.7 %all-gather.2.cloned.1.call-start = ((), (), s32[]{:S(2)}) async-start(), calls=%async_computation.1 | async-start | bytes 4259840 | tf_op jit(solution)/shard_map/all_gather | solution.py:23
  7.3 414.8 %reduce-scatter.2.cloned.1.call-start = ((), (), s32[]{:S(2)}) async-start(), calls=%async_computation.2 | async-start | bytes 1114112 | tf_op jit(solution)/shard_map/reduce_scatter | solution.py:28
Sparse Core Ops, SparseCore 0:
  13.2 219.0 all-gather.1
  238.3 183.6 reduce-scatter.1
where the time goes:
time: 432 us
  waiting for transfers between devices  409 us (95%)
  between operations  13.5 us (3%)
  local copies, waits for them, and re-layouts  4.38 us (1%)
    all_gather x1, waiting for transfers between devices, local(): gathered = lax.all_gather(current, 'wide', axis=0, tiled=True)  224 us
    reduce_scatter x1, waiting for transfers between devices, local(): lax.psum_scatter(partial_sum.reshape(panel_blocks * width, labels).astype...  184 us
  transfers between devices with their start and end apart: 2, of which 2 were waited for; matrix products, arithmetic and copies ran while one was open for 0% of the time, Pallas kernels for 0%

commit v1 on v0

v1 whole, which is shorter than its diff:
```python
import functools

import jax
import jax.numpy as jnp
from jax import lax
from jax.experimental import pallas as pl
from jax.experimental.pallas import tpu as pltpu
from jax.sharding import Mesh, PartitionSpec as P

WIDE = ("zh", "x", "y", "c")
PLANE = ("x", "y")
HALF, SIDE, LINE = 2, 4, 16
N_PLANE = SIDE * SIDE


def swap(value, axis):
    return lax.ppermute(value, axis, [(0, 1), (1, 0)])


def exchange(value, step):
    return lax.ppermute(value, "zl", [(i, i ^ step) for i in range(LINE)])


def plane_gather(value):
    spread = jnp.broadcast_to(value[None], (N_PLANE,) + value.shape)
    return lax.all_to_all(spread, PLANE, 0, 0)


def product_kernel(where, index, values, s00, s01, s10, s11, out, picked, sems):
    count = values.shape[0]
    width = values.shape[1]
    for k in range(count):
        for code, source in enumerate((s00, s01, s10, s11)):

            @pl.when(where[k] == code)
            def _():
                start = pl.multiple_of(index[k] * width, width)
                pltpu.make_async_copy(
                    source.at[pl.ds(start, width)], picked.at[k], sems.at[k]
                ).start()

    for k in range(count):
        pltpu.make_async_copy(s00.at[pl.ds(0, width)], picked.at[k], sems.at[k]).wait()
        out[k] = jnp.dot(
            values[k], picked[k], preferred_element_type=jnp.float32
        ).astype(out.dtype)


def products(where, index, values, sources):
    count, width, _ = values.shape
    labels = sources[0].shape[-1]
    smem = pl.BlockSpec(memory_space=pltpu.SMEM)
    vmem = pl.BlockSpec(memory_space=pltpu.VMEM)
    anywhere = pl.BlockSpec(memory_space=pl.ANY)
    return pl.pallas_call(
        product_kernel,
        out_shape=jax.ShapeDtypeStruct((count, width, labels), jnp.bfloat16),
        in_specs=[smem, smem, vmem] + [anywhere] * 4,
        out_specs=vmem,
        scratch_shapes=[
            pltpu.VMEM((count, width, labels), jnp.bfloat16),
            pltpu.SemaphoreType.DMA((count,)),
        ],
        cost_estimate=pl.CostEstimate(
            flops=2 * count * width * width * labels,
            bytes_accessed=6 * count * width * labels,
            transcendentals=0,
        ),
        name="products",
    )(where, index, values, *sources)


def collect_kernel(slot, mine, theirs, out, total):
    count = mine.shape[0]
    slots = out.shape[0]
    total[...] = jnp.zeros_like(total)
    for side, source in enumerate((mine, theirs)):
        for k in range(count):
            place = slot[side * count + k]

            @pl.when(place < slots)
            def _():
                total[place] += source[k].astype(jnp.float32)

    out[...] = total[...].astype(out.dtype)


def collect(slot, mine, theirs, slots):
    count, width, labels = mine.shape
    smem = pl.BlockSpec(memory_space=pltpu.SMEM)
    vmem = pl.BlockSpec(memory_space=pltpu.VMEM)
    return pl.pallas_call(
        collect_kernel,
        out_shape=jax.ShapeDtypeStruct((slots, width, labels), jnp.bfloat16),
        in_specs=[smem, vmem, vmem],
        out_specs=vmem,
        scratch_shapes=[pltpu.VMEM((slots, width, labels), jnp.float32)],
        cost_estimate=pl.CostEstimate(
            flops=2 * count * width * labels,
            bytes_accessed=(4 * count + 2 * slots) * width * labels,
            transcendentals=0,
        ),
        name="collect",
    )(slot, mine, theirs)


def local(state, block_values, block_rows, block_cols, anchor_ids, anchor_class):
    doc_dev, labels = state.shape
    width = block_values.shape[2]
    per_dev = doc_dev // width
    values = block_values[:, 0]
    cols = block_cols[:, 0]
    rows = block_rows[:, 0]
    zh, core, line = (lax.axis_index(a) for a in ("zh", "c", "zl"))
    bits = [(line // s) % 2 for s in (1, 2, 4, 8)]

    far = swap(state, "zh")
    near_own = plane_gather(state).reshape(-1, labels)
    their_rows = exchange(rows, 1)
    far_own = plane_gather(far).reshape(-1, labels)
    near_other = swap(near_own, "c")
    far_other = swap(far_own, "c")

    owner_dev, inner = cols // per_dev, cols % per_dev
    col_core = owner_dev % 2
    col_plane = (owner_dev // 2) % N_PLANE
    col_half = owner_dev // (2 * N_PLANE)
    where = 2 * (col_half != zh).astype(jnp.int32) + (col_core != core).astype(jnp.int32)
    index = col_plane * per_dev + inner
    mine = products(where, index, values, (near_own, near_other, far_own, far_other))

    both = jnp.concatenate([rows, their_rows])
    owner, inner = both // per_dev, both % per_dev
    b = [(owner // s) % 2 for s in (1, 2, 4, 8)]
    slot = ((b[1] * 2 + b[2]) * 2 + b[3]) * per_dev + inner
    slots = LINE // 2 * per_dev
    slot = jnp.where(b[0] == bits[0], slot, slots)
    theirs = exchange(mine, 1)
    held = collect(slot, mine, theirs, slots)
    for step, bit in ((2, bits[1]), (4, bits[2]), (8, bits[3])):
        halves = held.reshape((2, held.shape[0] // 2) + held.shape[1:])
        keep = lax.dynamic_index_in_dim(halves, bit, 0, keepdims=False)
        send = lax.dynamic_index_in_dim(halves, 1 - bit, 0, keepdims=False)
        got = exchange(send, step)
        held = keep.astype(jnp.float32) + got.astype(jnp.float32)
        if step < 8:
            held = held.astype(jnp.bfloat16)
    sums = held.reshape(doc_dev, labels)

    first_row = lax.axis_index(WIDE + ("zl",)) * doc_dev
    local_ids = anchor_ids - first_row
    match = local_ids[:, None] == jnp.arange(doc_dev, dtype=jnp.int32)[None, :]
    match = match.astype(jnp.float32)
    anchored = jnp.sum(match, axis=0) > 0.5
    fixed = jnp.dot(match.T, jax.nn.one_hot(anchor_class, labels, dtype=jnp.float32))
    total = sums + state.astype(jnp.float32)
    spread = total / jnp.sum(total, axis=-1, keepdims=True)
    spread = jnp.where(anchored[:, None], fixed, spread)
    return spread.astype(jnp.bfloat16)


def solution(mesh):
    shape = (HALF, SIDE, SIDE, 2, LINE)
    fine = Mesh(mesh.devices.reshape(shape), WIDE + ("zl",))
    every = WIDE + ("zl",)
    in_specs = (
        P(every, None),
        P(WIDE, "zl", None, None),
        P(WIDE, "zl"),
        P(WIDE, "zl"),
        P(every),
        P(every),
    )
    return jax.shard_map(
        local, mesh=fine, in_specs=in_specs, out_specs=P(every, None), check_vma=False
    )
```

time: 432 us -> 153 us (0.35)
  the two profiles are of different devices: /device:TPU:12 before, /device:TPU:1 now
where the time goes in v1:
time: 153 us; the launch traced here: 152 us
  starting transfers between devices  93 us (61%)
  waiting for transfers between devices  42.8 us (28%)
  local copies, waits for them, and re-layouts  6.74 us (4%)
  Pallas kernels  5.78 us (4%)
  other arithmetic  2.07 us (1%)
    ppermute x3, starting transfers between devices, swap(): return lax.ppermute(value, axis, [(0, 1), (1, 0)])  43.4 us
    ppermute x5, starting transfers between devices, exchange(): return lax.ppermute(value, 'zl', [(i, i ^ step) for i in range(LINE)])  35.3 us
    ppermute x5, waiting for transfers between devices, exchange(): return lax.ppermute(value, 'zl', [(i, i ^ step) for i in range(LINE)])  34.9 us
    all_to_all x2, starting transfers between devices, plane_gather(): return lax.all_to_all(spread, PLANE, 0, 0)  14.3 us
    all_to_all x2, waiting for transfers between devices, plane_gather(): return lax.all_to_all(spread, PLANE, 0, 0)  5.33 us
    pallas_call x1, Pallas kernels, products(): pl.pallas_call(product_kernel, out_shape=jax.ShapeDtypeStruct((count, wid...  3.68 us
    broadcast_in_dim x2, local copies, waits for them, and re-layouts, plane_gather(): spread = jnp.broadcast_to(value[None], (N_PLANE,) + value.shape)  3.37 us
  transfers between devices with their start and end apart: 10, of which 7 were waited for; matrix products, arithmetic and copies ran while one was open for 1% of the time, Pallas kernels for 0%

profile of v1, /device:TPU:1, one launch (start us, length us, event | category | flops | bytes accessed | tf_op | source)
XLA Modules:
  0.0 151.8 jit_solution(3403628414717555944)
XLA Ops:
  0.0 2.0 %broadcast_in_dim.17 = bf16[16,256,128]{2,1,0:T(8,128)(2,1)} broadcast(bf16[256,128]{1,0:T(8,128)(2,1)} %param.6), dimensions={1,2} | broadcast | bytes 1114112 | tf_op jit(solution)/shard_map/broadcast_in_dim | solution.py:25
  2.0 7.7 %all-to-all-start = ((bf16[16,256,128]{2,1,0:T(8,128)(2,1)}), bf16[16,256,128]{2,1,0:T(8,128)(2,1)S(1)}, u32[]{:S(2)}, u32[]{:S(2)}) async-start(bf16[16,256,128]{2,1,0:T(8,128)(2,1)} %broadcast_in_dim.17), calls=%async_computation | async-start | bytes 2097152 | tf_op jit(solution)/shard_map/all_to_all | solution.py:26
  9.8 28.7 %collective-permute-start.2 = (bf16[256,128]{1,0:T(8,128)(2,1)S(1)}, bf16[256,128]{1,0:T(8,128)(2,1)S(1)}, u32[]{:S(2)}, u32[]{:S(2)}) collective-permute-start(bf16[256,128]{1,0:T(8,128)(2,1)S(1)} %copy-done.4), channel_id=1, source_target_pairs={{0,512},{512,0},{1,513},{513,1},{2,514},{514,2},{3,515},{515,3},{4... | collective-permute-start | bytes 196616 | tf_op jit(solution)/shard_map/ppermute | solution.py:17
  38.5 2.0 %collective-permute-done.2 = bf16[256,128]{1,0:T(8,128)(2,1)S(1)} collective-permute-done((bf16[256,128]{1,0:T(8,128)(2,1)S(1)}, bf16[256,128]{1,0:T(8,128)(2,1)S(1)}, u32[]{:S(2)}, u32[]{:S(2)}) %collective-permute-start.2) | collective-permute-done | bytes 65568 | tf_op jit(solution)/shard_map/ppermute | solution.py:17
  40.5 1.3 broadcast_in_dim.18
  41.8 6.6 %all-to-all-start.1 = ((bf16[16,256,128]{2,1,0:T(8,128)(2,1)}), bf16[16,256,128]{2,1,0:T(8,128)(2,1)S(1)}, u32[]{:S(2)}, u32[]{:S(2)}) async-start(bf16[16,256,128]{2,1,0:T(8,128)(2,1)} %broadcast_in_dim.18), calls=%async_computation.1 | async-start | bytes 2097152 | tf_op jit(solution)/shard_map/all_to_all | solution.py:26
  48.4 6.6 %collective-permute-start.1 = (bf16[4096,128]{1,0:T(8,128)(2,1)S(1)}, bf16[4096,128]{1,0:T(8,128)(2,1)S(1)}, u32[]{:S(2)}, u32[]{:S(2)}) collective-permute-start(bf16[4096,128]{1,0:T(8,128)(2,1)S(1)} %bitcast.44), channel_id=1, source_target_pairs={{0,16},{16,0},{1,17},{17,1},{2,18},{18,2},{3,19},{19,3},{4,20},{20... | collective-permute-start | bytes 3145736 | tf_op jit(solution)/shard_map/ppermute | solution.py:17
  55.1 5.3 %all-to-all-done.1 = bf16[16,256,128]{2,1,0:T(8,128)(2,1)S(1)} async-done(((bf16[16,256,128]{2,1,0:T(8,128)(2,1)}), bf16[16,256,128]{2,1,0:T(8,128)(2,1)S(1)}, u32[]{:S(2)}, u32[]{:S(2)}) %all-to-all-start.1) | async-done | bytes 1048608 | tf_op jit(solution)/shard_map/all_to_all | solution.py:26
  60.4 8.1 %collective-permute-start.3 = (bf16[4096,128]{1,0:T(8,128)(2,1)S(1)}, bf16[4096,128]{1,0:T(8,128)(2,1)}, u32[]{:S(2)}, u32[]{:S(2)}) collective-permute-start(bf16[4096,128]{1,0:T(8,128)(2,1)S(1)} %bitcast.46), channel_id=1, source_target_pairs={{0,16},{16,0},{1,17},{17,1},{2,18},{18,2},{3,19},{19,3},{4,20},{20... | collective-permute-start | bytes 3145736 | tf_op jit(solution)/shard_map/ppermute | solution.py:17
  68.5 0.6 copy-done.7
  69.2 0.5 fusion.9
  69.7 0.6 fusion.11.where
  70.3 0.6 collective-permute-done.3.s11
  70.9 0.4 copy-done.3
  71.3 3.7 %products.1.mine = bf16[8,128,128]{2,1,0:T(8,128)(2,1)} custom-call(s32[8]{0:T(128)} %fusion.11.where, s32[8]{0:T(128)} %get-tuple-element.5.index, bf16[8,128,128]{2,1,0:T(8,128)(2,1)} %bitcast.54, bf16[4096,128]{1,0:T(8,128)(2,1)} %bitcast.45, bf16[4096,128]{1,0:T(8,128)(2,1)} %copy-done.3, bf16[4096,128]{1,0:T(8,128)(2,1)} %bitcast.47, ...), custom_call_target="tpu_custom_call" | custom-call | flops 33554432 | bytes 786432 | tf_op jit(solution)/shard_map/products/pallas_call | solution.py:55
  75.0 3.5 %collective-permute-start.4 = (bf16[8,128,128]{2,1,0:T(8,128)(2,1)}, bf16[8,128,128]{2,1,0:T(8,128)(2,1)S(1)}, u32[]{:S(2)}, u32[]{:S(2)}) collective-permute-start(bf16[8,128,128]{2,1,0:T(8,128)(2,1)} %products.1.mine), channel_id=1, source_target_pairs={{0,1},{1,0},{2,3},{3,2},{4,5},{5,4},{6,7},{7,6},{8,9},{9,8},{10,11... | collective-permute-start | bytes 786440 | tf_op jit(solution)/shard_map/ppermute | solution.py:21
  78.5 1.9 %collective-permute-start = (s32[8]{0:T(128)S(1)}, s32[8]{0:T(128)S(1)}, u32[]{:S(2)}, u32[]{:S(2)}) collective-permute-start(s32[8]{0:T(128)S(1)} %bitcast.55), channel_id=1, source_target_pairs={{0,1},{1,0},{2,3},{3,2},{4,5},{5,4},{6,7},{7,6},{8,9},{9,8},{10,11... | collective-permute-start | bytes 104 | tf_op jit(solution)/shard_map/ppermute | solution.py:21
  80.4 4.8 %collective-permute-done = s32[8]{0:T(128)S(1)} collective-permute-done((s32[8]{0:T(128)S(1)}, s32[8]{0:T(128)S(1)}, u32[]{:S(2)}, u32[]{:S(2)}) %collective-permute-start) | collective-permute-done | bytes 64 | tf_op jit(solution)/shard_map/ppermute | solution.py:21
  85.2 0.6 compare_select_fusion.9.slot
  85.9 0.7 copy-done.5
  86.6 2.1 %collect.1 = bf16[16,128,128]{2,1,0:T(8,128)(2,1)} custom-call(s32[16]{0:T(128)} %compare_select_fusion.9.slot, bf16[8,128,128]{2,1,0:T(8,128)(2,1)} %products.1.mine, bf16[8,128,128]{2,1,0:T(8,128)(2,1)} %copy-done.5), custom_call_target="tpu_custom_call" | custom-call | flops 262144 | bytes 1048576 | tf_op jit(solution)/shard_map/collect/pallas_call | solution.py:92
  88.7 1.0 dynamic-slice_bitcast_fusion
  89.7 2.7 %collective-permute-start.5 = (bf16[8,128,128]{2,1,0:T(8,128)(2,1)S(1)}, bf16[8,128,128]{2,1,0:T(8,128)(2,1)S(1)}, u32[]{:S(2)}, u32[]{:S(2)}) collective-permute-start(bf16[8,128,128]{2,1,0:T(8,128)(2,1)S(1)} %dynamic-slice_bitcast_fusion), channel_id=1, source_target_pairs={{0,2},{1,3},{2,0},{3,1},{4,6},{5,7},{6,4},{7,5},{8,10},{9,11},{10,... | collective-permute-start | bytes 786440 | tf_op jit(solution)/shard_map/ppermute | solution.py:21
  92.5 12.7 %collective-permute-done.5 = bf16[8,128,128]{2,1,0:T(8,128)(2,1)S(1)} collective-permute-done((bf16[8,128,128]{2,1,0:T(8,128)(2,1)S(1)}, bf16[8,128,128]{2,1,0:T(8,128)(2,1)S(1)}, u32[]{:S(2)}, u32[]{:S(2)}) %collective-permute-start.5) | collective-permute-done | bytes 262176 | tf_op jit(solution)/shard_map/ppermute | solution.py:21
  105.4 9.2 %collective-permute-start.6 = (bf16[4,128,128]{2,1,0:T(8,128)(2,1)S(1)}, bf16[4,128,128]{2,1,0:T(8,128)(2,1)S(1)}, u32[]{:S(2)}, u32[]{:S(2)}) collective-permute-start(bf16[4,128,128]{2,1,0:T(8,128)(2,1)S(1)} %dynamic-slice_bitcast_fusion.1), channel_id=1, source_target_pairs={{0,4},{1,5},{2,6},{3,7},{4,0},{5,1},{6,2},{7,3},{8,12},{9,13},{10,... | collective-permute-start | bytes 393224 | tf_op jit(solution)/shard_map/ppermute | solution.py:21
  114.6 0.1 convert_reduce_fusion
  114.7 10.5 %collective-permute-done.6 = bf16[4,128,128]{2,1,0:T(8,128)(2,1)S(1)} collective-permute-done((bf16[4,128,128]{2,1,0:T(8,128)(2,1)S(1)}, bf16[4,128,128]{2,1,0:T(8,128)(2,1)S(1)}, u32[]{:S(2)}, u32[]{:S(2)}) %collective-permute-start.6) | collective-permute-done | bytes 131104 | tf_op jit(solution)/shard_map/ppermute | solution.py:21
  125.3 18.0 %collective-permute-start.7 = (bf16[2,128,128]{2,1,0:T(8,128)(2,1)S(1)}, bf16[2,128,128]{2,1,0:T(8,128)(2,1)S(1)}, u32[]{:S(2)}, u32[]{:S(2)}) collective-permute-start(bf16[2,128,128]{2,1,0:T(8,128)(2,1)S(1)} %dynamic-slice_bitcast_fusion.2), channel_id=1, source_target_pairs={{0,8},{1,9},{2,10},{3,11},{4,12},{5,13},{6,14},{7,15},{8,0},{9,1},... | collective-permute-start | bytes 196616 | tf_op jit(solution)/shard_map/ppermute | solution.py:21
  143.3 6.8 %collective-permute-done.7 = bf16[2,128,128]{2,1,0:T(8,128)(2,1)S(1)} collective-permute-done((bf16[2,128,128]{2,1,0:T(8,128)(2,1)S(1)}, bf16[2,128,128]{2,1,0:T(8,128)(2,1)S(1)}, u32[]{:S(2)}, u32[]{:S(2)}) %collective-permute-start.7) | collective-permute-done | bytes 65568 | tf_op jit(solution)/shard_map/ppermute | solution.py:21
  150.2 0.1 fusion.2
  150.3 0.5 copy-done.9
  150.8 0.9 select_convert_fusion
  (26 shorter events, 0.2 us)
Async XLA Ops:
  2.0 7.7 %copy-start.4 = (bf16[256,128]{1,0:T(8,128)(2,1)S(1)}, bf16[256,128]{1,0:T(8,128)(2,1)}, u32[]{:S(2)}) copy-start(bf16[256,128]{1,0:T(8,128)(2,1)} %param.6) | copy-start | bytes 196612
  2.0 38.4 %all-to-all-start = ((bf16[16,256,128]{2,1,0:T(8,128)(2,1)}), bf16[16,256,128]{2,1,0:T(8,128)(2,1)S(1)}, u32[]{:S(2)}, u32[]{:S(2)}) async-start(bf16[16,256,128]{2,1,0:T(8,128)(2,1)} %broadcast_in_dim.17), calls=%async_computation | async-start | bytes 2097152 | tf_op jit(solution)/shard_map/all_to_all | solution.py:26
  9.8 30.7 %collective-permute-start.2 = (bf16[256,128]{1,0:T(8,128)(2,1)S(1)}, bf16[256,128]{1,0:T(8,128)(2,1)S(1)}, u32[]{:S(2)}, u32[]{:S(2)}) collective-permute-start(bf16[256,128]{1,0:T(8,128)(2,1)S(1)} %copy-done.4), channel_id=1, source_target_pairs={{0,512},{512,0},{1,513},{513,1},{2,514},{514,2},{3,515},{515,3},{4... | collective-permute-start | bytes 196616 | tf_op jit(solution)/shard_map/ppermute | solution.py:17
  40.5 8.0 %copy-start = (bf16[16,256,128]{2,1,0:T(8,128)(2,1)}, bf16[16,256,128]{2,1,0:T(8,128)(2,1)S(1)}, u32[]{:S(2)}) copy-start(bf16[16,256,128]{2,1,0:T(8,128)(2,1)S(1)} %all-to-all-done) | copy-start | bytes 3145732
  41.8 18.6 %all-to-all-start.1 = ((bf16[16,256,128]{2,1,0:T(8,128)(2,1)}), bf16[16,256,128]{2,1,0:T(8,128)(2,1)S(1)}, u32[]{:S(2)}, u32[]{:S(2)}) async-start(bf16[16,256,128]{2,1,0:T(8,128)(2,1)} %broadcast_in_dim.18), calls=%async_computation.1 | async-start | bytes 2097152 | tf_op jit(solution)/shard_map/all_to_all | solution.py:26
  48.4 21.9 %collective-permute-start.1 = (bf16[4096,128]{1,0:T(8,128)(2,1)S(1)}, bf16[4096,128]{1,0:T(8,128)(2,1)S(1)}, u32[]{:S(2)}, u32[]{:S(2)}) collective-permute-start(bf16[4096,128]{1,0:T(8,128)(2,1)S(1)} %bitcast.44), channel_id=1, source_target_pairs={{0,16},{16,0},{1,17},{17,1},{2,18},{18,2},{3,19},{19,3},{4,20},{20... | collective-permute-start | bytes 3145736 | tf_op jit(solution)/shard_map/ppermute | solution.py:17
  60.4 10.5 %copy-start.1 = (bf16[16,256,128]{2,1,0:T(8,128)(2,1)}, bf16[16,256,128]{2,1,0:T(8,128)(2,1)S(1)}, u32[]{:S(2)}) copy-start(bf16[16,256,128]{2,1,0:T(8,128)(2,1)S(1)} %all-to-all-done.1) | copy-start | bytes 3145732
  60.4 10.5 %collective-permute-start.3 = (bf16[4096,128]{1,0:T(8,128)(2,1)S(1)}, bf16[4096,128]{1,0:T(8,128)(2,1)}, u32[]{:S(2)}, u32[]{:S(2)}) collective-permute-start(bf16[4096,128]{1,0:T(8,128)(2,1)S(1)} %bitcast.46), channel_id=1, source_target_pairs={{0,16},{16,0},{1,17},{17,1},{2,18},{18,2},{3,19},{19,3},{4,20},{20... | collective-permute-start | bytes 3145736 | tf_op jit(solution)/shard_map/ppermute | solution.py:17
  68.5 0.7 copy-start.7
  70.3 1.0 copy-start.3
  75.0 3.5 %copy-start.6 = (s32[8,1]{0,1:T(1,128)S(1)}, s32[8,1]{0,1:T(1,128)}, u32[]{:S(2)}) copy-start(s32[8,1]{0,1:T(1,128)} %param.8) | copy-start | bytes 100
  75.0 10.9 %collective-permute-start.4 = (bf16[8,128,128]{2,1,0:T(8,128)(2,1)}, bf16[8,128,128]{2,1,0:T(8,128)(2,1)S(1)}, u32[]{:S(2)}, u32[]{:S(2)}) collective-permute-start(bf16[8,128,128]{2,1,0:T(8,128)(2,1)} %products.1.mine), channel_id=1, source_target_pairs={{0,1},{1,0},{2,3},{3,2},{4,5},{5,4},{6,7},{7,6},{8,9},{9,8},{10,11... | collective-permute-start | bytes 786440 | tf_op jit(solution)/shard_map/ppermute | solution.py:21
  78.5 6.8 %collective-permute-start = (s32[8]{0:T(128)S(1)}, s32[8]{0:T(128)S(1)}, u32[]{:S(2)}, u32[]{:S(2)}) collective-permute-start(s32[8]{0:T(128)S(1)} %bitcast.55), channel_id=1, source_target_pairs={{0,1},{1,0},{2,3},{3,2},{4,5},{5,4},{6,7},{7,6},{8,9},{9,8},{10,11... | collective-permute-start | bytes 104 | tf_op jit(solution)/shard_map/ppermute | solution.py:21
  85.9 0.7 copy-start.5
  88.7 16.6 %copy-start.2 = (bf16[16,128,128]{2,1,0:T(8,128)(2,1)S(1)}, bf16[16,128,128]{2,1,0:T(8,128)(2,1)}, u32[]{:S(2)}) copy-start(bf16[16,128,128]{2,1,0:T(8,128)(2,1)} %collect.1) | copy-start | bytes 1572868
  89.7 15.5 %collective-permute-start.5 = (bf16[8,128,128]{2,1,0:T(8,128)(2,1)S(1)}, bf16[8,128,128]{2,1,0:T(8,128)(2,1)S(1)}, u32[]{:S(2)}, u32[]{:S(2)}) collective-permute-start(bf16[8,128,128]{2,1,0:T(8,128)(2,1)S(1)} %dynamic-slice_bitcast_fusion), channel_id=1, source_target_pairs={{0,2},{1,3},{2,0},{3,1},{4,6},{5,7},{6,4},{7,5},{8,10},{9,11},{10,... | collective-permute-start | bytes 786440 | tf_op jit(solution)/shard_map/ppermute | solution.py:21
  105.3 9.2 %copy-start.8 = (s32[8]{0:T(128)S(1)}, s32[8]{0:T(128)}, u32[]{:S(2)}) copy-start(s32[8]{0:T(128)} %param.10) | copy-start | bytes 100
  105.4 19.9 %collective-permute-start.6 = (bf16[4,128,128]{2,1,0:T(8,128)(2,1)S(1)}, bf16[4,128,128]{2,1,0:T(8,128)(2,1)S(1)}, u32[]{:S(2)}, u32[]{:S(2)}) collective-permute-start(bf16[4,128,128]{2,1,0:T(8,128)(2,1)S(1)} %dynamic-slice_bitcast_fusion.1), channel_id=1, source_target_pairs={{0,4},{1,5},{2,6},{3,7},{4,0},{5,1},{6,2},{7,3},{8,12},{9,13},{10,... | collective-permute-start | bytes 393224 | tf_op jit(solution)/shard_map/ppermute | solution.py:21
  125.3 24.8 %collective-permute-start.7 = (bf16[2,128,128]{2,1,0:T(8,128)(2,1)S(1)}, bf16[2,128,128]{2,1,0:T(8,128)(2,1)S(1)}, u32[]{:S(2)}, u32[]{:S(2)}) collective-permute-start(bf16[2,128,128]{2,1,0:T(8,128)(2,1)S(1)} %dynamic-slice_bitcast_fusion.2), channel_id=1, source_target_pairs={{0,8},{1,9},{2,10},{3,11},{4,12},{5,13},{6,14},{7,15},{8,0},{9,1},... | collective-permute-start | bytes 196616 | tf_op jit(solution)/shard_map/ppermute | solution.py:21
  150.2 0.7 copy-start.9

commit v2 on v1

v2 whole, which is shorter than its diff:
```python
import jax
import jax.numpy as jnp
from jax import lax
from jax.experimental import pallas as pl
from jax.experimental.pallas import tpu as pltpu
from jax.sharding import Mesh, PartitionSpec as P

WIDE = ("zh", "x", "y", "c")
PLANE = ("x", "y")
HALF, SIDE, LINE = 2, 4, 16
N_PLANE = SIDE * SIDE
SMEM = pl.BlockSpec(memory_space=pltpu.SMEM)
VMEM = pl.BlockSpec(memory_space=pltpu.VMEM)


def cost(flops, nbytes):
    return pl.CostEstimate(flops=flops, bytes_accessed=nbytes, transcendentals=0)


def swap(value, axis):
    return lax.ppermute(value, axis, [(0, 1), (1, 0)])


def exchange(value, step):
    return lax.ppermute(value, "zl", [(i, i ^ step) for i in range(LINE)])


def spread(value):
    return jnp.broadcast_to(value[None], (N_PLANE,) + value.shape)


def plane_exchange(value):
    return lax.all_to_all(value, PLANE, 0, 0)


def product_kernel(facts, values, s00, s01, s10, s11, first, second, picked):
    count, width = values.shape[:2]
    half = width // 2
    for k in range(count):
        start = pl.multiple_of(facts[count + k] * width, width)
        for number, source in enumerate((s00, s01, s10, s11)):

            @pl.when(facts[k] == number)
            def _():
                picked[k] = source[pl.ds(start, width), :]

    for k in range(count):
        out = jnp.dot(values[k], picked[k], preferred_element_type=jnp.float32)
        first[k] = out[:half].astype(first.dtype)
        second[k] = out[half:].astype(second.dtype)


def products(facts, values, sources):
    count, width, _ = values.shape
    labels = sources[0].shape[-1]
    part = jax.ShapeDtypeStruct((count, width // 2, labels), jnp.bfloat16)
    return pl.pallas_call(
        product_kernel,
        out_shape=(part, part),
        in_specs=[SMEM] + [VMEM] * 5,
        out_specs=(VMEM, VMEM),
        scratch_shapes=[pltpu.VMEM((count, width, labels), jnp.bfloat16)],
        compiler_params=pltpu.CompilerParams(vmem_limit_bytes=16 * 2**20),
        cost_estimate=cost(2 * count * width * width * labels, 6 * count * width * labels),
        name="products",
    )(facts, values, *sources)


def collect_kernel(slot, mine, theirs, keep, send, total):
    count = mine.shape[0]
    slots = keep.shape[0]
    total[...] = jnp.zeros_like(total)
    for side, source in enumerate((mine, theirs)):
        for k in range(count):
            place = slot[side * count + k]

            @pl.when(place < 2 * slots)
            def _():
                total[place] += source[k].astype(jnp.float32)

    send[...] = total[slots:].astype(send.dtype)
    keep[...] = total[:slots].astype(keep.dtype)


def collect(slot, mine, theirs, slots):
    count, rows, labels = mine.shape
    part = jax.ShapeDtypeStruct((slots, rows, labels), jnp.bfloat16)
    return pl.pallas_call(
        collect_kernel,
        out_shape=(part, part),
        in_specs=[SMEM, VMEM, VMEM],
        out_specs=(VMEM, VMEM),
        scratch_shapes=[pltpu.VMEM((2 * slots, rows, labels), jnp.float32)],
        cost_estimate=cost(2 * count * rows * labels, (4 * count + 4 * slots) * rows * labels),
        name="collect",
    )(slot, mine, theirs)


def local(state, block_values, block_rows, block_cols, anchor_ids, anchor_class):
    doc_dev, labels = state.shape
    width = block_values.shape[2]
    per_dev = doc_dev // width
    values = block_values[:, 0]
    cols = block_cols[:, 0]
    rows = block_rows[:, 0]
    zh, core, line = (lax.axis_index(a) for a in ("zh", "c", "zl"))
    bits = {s: (line // s) % 2 for s in (1, 2, 4, 8)}

    owner_dev, inner = cols // per_dev, cols % per_dev
    col_core = owner_dev % 2
    col_plane = (owner_dev // 2) % N_PLANE
    col_half = owner_dev // (2 * N_PLANE)
    where = 2 * (col_half != zh).astype(jnp.int32) + (col_core != core).astype(jnp.int32)
    facts = jnp.concatenate([where, col_plane * per_dev + inner])

    copies = spread(state)
    from_second = lax.ppermute(state, "zh", [(1, 0)])
    near_own = lax.cond(zh == 0, plane_exchange, lambda value: value, copies)
    again, near_own = lax.optimization_barrier((state, near_own))
    from_first = lax.ppermute(again, "zh", [(0, 1)])
    near_own = lax.cond(zh == 1, plane_exchange, lambda value: value, near_own)
    far = jnp.where(zh == 0, from_second, from_first)
    rows_late, near_own = lax.optimization_barrier((rows, near_own))
    both = jnp.concatenate([rows, exchange(rows_late, 1)])
    owner, inner = both // per_dev, both % per_dev
    b = {s: (owner // s) % 2 for s in (1, 2, 4, 8)}
    slots = LINE // 4 * per_dev
    slot = (b[4] * 2 + b[8]) * per_dev + inner
    slot = slot + jnp.where(b[2] == bits[2], 0, slots)
    slot = jnp.where(b[1] == bits[1], slot, 2 * slots)
    far_own = plane_exchange(spread(far)).reshape(-1, labels)
    far_own, facts, slot = lax.optimization_barrier((far_own, facts, slot))
    near_own = near_own.reshape(-1, labels)
    near_other = swap(near_own, "c")
    far_other = swap(far_own, "c")
    mine = products(facts, values, (near_own, near_other, far_own, far_other))

    theirs = [exchange(part, 1) for part in mine]
    held = [collect(slot, *parts, slots) for parts in zip(mine, theirs)]
    got = [exchange(send, 2) for _, send in held]

    def halve(keep, came, step):
        pair = (2, keep.shape[0] // 2) + keep.shape[1:]
        keep, came = keep.reshape(pair), came.reshape(pair)
        bit = bits[step]

        def side(index):
            one = lax.dynamic_index_in_dim(keep, index, 0, keepdims=False)
            two = lax.dynamic_index_in_dim(came, index, 0, keepdims=False)
            return one + two

        return side(bit), side(1 - bit)

    held = [halve(keep, came, 4) for (keep, _), came in zip(held, got)]
    got = [exchange(send, 4) for _, send in held]
    held = [halve(keep, came, 8) for (keep, _), came in zip(held, got)]
    keep, send = (jnp.concatenate(parts, axis=1) for parts in zip(*held))
    sums = keep.astype(jnp.float32) + exchange(send, 8).astype(jnp.float32)
    sums = sums.reshape(doc_dev, labels)

    first_row = lax.axis_index(WIDE + ("zl",)) * doc_dev
    local_ids = anchor_ids - first_row
    match = local_ids[:, None] == jnp.arange(doc_dev, dtype=jnp.int32)[None, :]
    match = match.astype(jnp.float32)
    anchored = jnp.sum(match, axis=0) > 0.5
    fixed = jnp.dot(match.T, jax.nn.one_hot(anchor_class, labels, dtype=jnp.float32))
    total = sums + state.astype(jnp.float32)
    result = total / jnp.sum(total, axis=-1, keepdims=True)
    result = jnp.where(anchored[:, None], fixed, result)
    return result.astype(jnp.bfloat16)


def solution(mesh):
    shape = (HALF, SIDE, SIDE, 2, LINE)
    every = WIDE + ("zl",)
    fine = Mesh(mesh.devices.reshape(shape), every)
    in_specs = (
        P(every, None),
        P(WIDE, "zl", None, None),
        P(WIDE, "zl"),
        P(WIDE, "zl"),
        P(every),
        P(every),
    )
    return jax.shard_map(
        local, mesh=fine, in_specs=in_specs, out_specs=P(every, None), check_vma=False
    )
```

time: 153 us -> 139 us (0.908)
  starting transfers between devices: 93 us -> 72.2 us
  blocking collectives: 0 us -> 19.2 us
  waiting for transfers between devices: 42.8 us -> 31.8 us
    ppermute x3 -> x2, starting transfers between devices: 43.4 us -> 9.72 us  [swap(): return lax.ppermute(value, axis, [(0, 1), (1, 0)])]
    all_to_all x0 -> x1, blocking collectives: none -> 19.2 us  [plane_exchange(): return lax.all_to_all(value, PLANE, 0, 0)]
    ppermute x5 -> x8, waiting for transfers between devices: 34.9 us -> 19.9 us  [exchange(): return lax.ppermute(value, 'zl', [(i, i ^ step) for i in range(LINE)])]
    ppermute x0 -> x2, starting transfers between devices: none -> 11.1 us  [the longest x1 9.86 us: local(): from_first = lax.ppermute(again, 'zh', [(0, 1)])]
    ppermute x5 -> x8, starting transfers between devices: 35.3 us -> 43.2 us  [exchange(): return lax.ppermute(value, 'zl', [(i, i ^ step) for i in range(LINE)])]
    all_to_all x2 -> x1, starting transfers between devices: 14.3 us -> 8.19 us  [plane_exchange(): return lax.all_to_all(value, PLANE, 0, 0)]
    ppermute x0 -> x2, waiting for transfers between devices: none -> 3.19 us  [the longest x1 3.19 us: local(): from_first = lax.ppermute(again, 'zh', [(0, 1)])]
    all_to_all x2 -> x1, waiting for transfers between devices: 5.33 us -> 6.4 us  [plane_exchange(): return lax.all_to_all(value, PLANE, 0, 0)]
  transfers between devices with their start and end apart: 10 -> 13, of which waited for: 7 -> 8; matrix products, arithmetic and copies ran while one was open for 1% -> 3% of each run, Pallas kernels for 0% -> 3%
where the time goes in v2:
time: 139 us
  starting transfers between devices  72.2 us (52%)
  waiting for transfers between devices  31.8 us (23%)
  blocking collectives  19.2 us (14%)
  local copies, waits for them, and re-layouts  7.62 us (5%)
  Pallas kernels  5.45 us (4%)
    ppermute x8, starting transfers between devices, exchange(): return lax.ppermute(value, 'zl', [(i, i ^ step) for i in range(LINE)])  43.2 us
    ppermute x8, waiting for transfers between devices, exchange(): return lax.ppermute(value, 'zl', [(i, i ^ step) for i in range(LINE)])  19.9 us
    all_to_all x1, blocking collectives, plane_exchange(): return lax.all_to_all(value, PLANE, 0, 0)  19.2 us
    ppermute x1, starting transfers between devices, local(): from_first = lax.ppermute(again, 'zh', [(0, 1)])  9.86 us
    ppermute x2, starting transfers between devices, swap(): return lax.ppermute(value, axis, [(0, 1), (1, 0)])  9.72 us
    all_to_all x1, starting transfers between devices, plane_exchange(): return lax.all_to_all(value, PLANE, 0, 0)  8.19 us
    all_to_all x1, waiting for transfers between devices, plane_exchange(): return lax.all_to_all(value, PLANE, 0, 0)  6.4 us
    pallas_call x2, Pallas kernels, collect(): pl.pallas_call(collect_kernel, out_shape=(part, part), in_specs=[SMEM, VM...  3.73 us
  transfers between devices with their start and end apart: 13, of which 8 were waited for; matrix products, arithmetic and copies ran while one was open for 3% of the time, Pallas kernels for 3%

profile of v2, /device:TPU:1, one launch (start us, length us, event | category | flops | bytes accessed | tf_op | source)
XLA Modules:
  0.0 138.7 jit_solution(2745149111081096251)
XLA Ops:
  0.0 1.3 collective-permute-start
  1.3 2.0 %broadcast_in_dim.26 = bf16[16,256,128]{2,1,0:T(8,128)(2,1)} broadcast(bf16[256,128]{1,0:T(8,128)(2,1)} %param.10), dimensions={1,2} | broadcast | bytes 1114112 | tf_op jit(solution)/shard_map/broadcast_in_dim | solution.py:29
  3.3 20.5 %conditional.2 = (bf16[16,256,128]{2,1,0:T(8,128)(2,1)}) conditional(s32[]{:T(128)} %convert_element_type.28, bf16[16,256,128]{2,1,0:T(8,128)(2,1)} %broadcast_in_dim.26, bf16[16,256,128]{2,1,0:T(8,128)(2,1)} %broadcast_in_dim.26), branch_computations={%region_1.2_spmd, %region_2.3_spmd} | conditional | bytes 4194312 | solution.py:118
  3.3 1.3 copy.11
  4.6 19.2 %all_to_all.13 = bf16[16,256,128]{2,1,0:T(8,128)(2,1)} all-to-all(bf16[16,256,128]{2,1,0:T(8,128)(2,1)S(1)} %copy.11), channel_id=1, replica_groups=mesh['zh'=2,'x'=4,'y'=4,'c'=2,'zl'=16] {'x','y'}, dimensions={0} | all-to-all | bytes 2097152 | tf_op jit(solution)/shard_map/cond/branch_1_fun/all_to_all | solution.py:33
  23.8 9.9 %collective-permute-start.1 = (bf16[256,128]{1,0:T(8,128)(2,1)S(1)}, bf16[256,128]{1,0:T(8,128)(2,1)S(1)}, u32[]{:S(2)}, u32[]{:S(2)}) collective-permute-start(bf16[256,128]{1,0:T(8,128)(2,1)S(1)} %copy-done.3), channel_id=1, source_target_pairs={{0,512},{1,513},{2,514},{3,515},{4,516},{5,517},{6,518},{7,519},{8... | collective-permute-start | bytes 196616 | tf_op jit(solution)/shard_map/ppermute | solution.py:120
  33.7 3.2 %collective-permute-done.1 = bf16[256,128]{1,0:T(8,128)(2,1)S(1)} collective-permute-done((bf16[256,128]{1,0:T(8,128)(2,1)S(1)}, bf16[256,128]{1,0:T(8,128)(2,1)S(1)}, u32[]{:S(2)}, u32[]{:S(2)}) %collective-permute-start.1) | collective-permute-done | bytes 65568 | tf_op jit(solution)/shard_map/ppermute | solution.py:120
  36.9 1.2 broadcast_in_dim.42
  38.1 8.2 %all-to-all-start.2 = ((bf16[16,256,128]{2,1,0:T(8,128)(2,1)}), bf16[16,256,128]{2,1,0:T(8,128)(2,1)S(1)}, u32[]{:S(2)}, u32[]{:S(2)}) async-start(bf16[16,256,128]{2,1,0:T(8,128)(2,1)} %broadcast_in_dim.42), calls=%async_computation.2 | async-start | bytes 2097152 | tf_op jit(solution)/shard_map/all_to_all | solution.py:33
  46.3 0.6 copy-done.9
  47.0 1.9 %collective-permute-start.2 = (s32[8]{0:T(128)S(1)}, s32[8]{0:T(128)S(1)}, u32[]{:S(2)}, u32[]{:S(2)}) collective-permute-start(s32[8]{0:T(128)S(1)} %bitcast.57), channel_id=1, source_target_pairs={{0,1},{1,0},{2,3},{3,2},{4,5},{5,4},{6,7},{7,6},{8,9},{9,8},{10,11... | collective-permute-start | bytes 104 | tf_op jit(solution)/shard_map/ppermute | solution.py:25
  48.9 4.7 %collective-permute-start.3 = (bf16[4096,128]{1,0:T(8,128)(2,1)}, bf16[4096,128]{1,0:T(8,128)(2,1)S(1)}, u32[]{:S(2)}, u32[]{:S(2)}) collective-permute-start(bf16[4096,128]{1,0:T(8,128)(2,1)} %bitcast.4.s00), channel_id=1, source_target_pairs={{0,16},{16,0},{1,17},{17,1},{2,18},{18,2},{3,19},{19,3},{4,20},{20... | collective-permute-start | bytes 3145736 | tf_op jit(solution)/shard_map/ppermute | solution.py:21
  55.0 6.4 %all-to-all-done.2 = bf16[16,256,128]{2,1,0:T(8,128)(2,1)S(1)} async-done(((bf16[16,256,128]{2,1,0:T(8,128)(2,1)}), bf16[16,256,128]{2,1,0:T(8,128)(2,1)S(1)}, u32[]{:S(2)}, u32[]{:S(2)}) %all-to-all-start.2) | async-done | bytes 1048608 | tf_op jit(solution)/shard_map/all_to_all | solution.py:33
  61.4 5.0 %collective-permute-start.4 = (bf16[4096,128]{1,0:T(8,128)(2,1)S(1)}, bf16[4096,128]{1,0:T(8,128)(2,1)S(1)}, u32[]{:S(2)}, u32[]{:S(2)}) collective-permute-start(bf16[4096,128]{1,0:T(8,128)(2,1)S(1)} %bitcast.46), channel_id=1, source_target_pairs={{0,16},{16,0},{1,17},{17,1},{2,18},{18,2},{3,19},{19,3},{4,20},{20... | collective-permute-start | bytes 3145736 | tf_op jit(solution)/shard_map/ppermute | solution.py:21
  66.4 2.3 %collective-permute-done.4.s11 = bf16[4096,128]{1,0:T(8,128)(2,1)S(1)} collective-permute-done((bf16[4096,128]{1,0:T(8,128)(2,1)S(1)}, bf16[4096,128]{1,0:T(8,128)(2,1)S(1)}, u32[]{:S(2)}, u32[]{:S(2)}) %collective-permute-start.4) | collective-permute-done | bytes 1048608 | tf_op jit(solution)/shard_map/ppermute | solution.py:21
  68.7 1.7 %products.1 = (bf16[8,64,128]{2,1,0:T(8,128)(2,1)S(1)}, bf16[8,64,128]{2,1,0:T(8,128)(2,1)S(1)}) custom-call(s32[16]{0:T(128)S(1)} %pad_add_fusion.facts, bf16[8,128,128]{2,1,0:T(8,128)(2,1)S(1)} %bitcast.48, bf16[4096,128]{1,0:T(8,128)(2,1)} %bitcast.4.s00, bf16[4096,128]{1,0:T(8,128)(2,1)S(1)} %collective-permute-done.3.s01, ...), custom_call_target="tpu_custom_call" | custom-call | flops 33554432 | bytes 786432 | tf_op jit(solution)/shard_map/products/pallas_call | solution.py:57
  70.5 1.9 %collective-permute-start.5 = (bf16[8,64,128]{2,1,0:T(8,128)(2,1)S(1)}, bf16[8,64,128]{2,1,0:T(8,128)(2,1)S(1)}, u32[]{:S(2)}, u32[]{:S(2)}) collective-permute-start(bf16[8,64,128]{2,1,0:T(8,128)(2,1)S(1)} %get-tuple-element.35.mine), channel_id=1, source_target_pairs={{0,1},{1,0},{2,3},{3,2},{4,5},{5,4},{6,7},{7,6},{8,9},{9,8},{10,11... | collective-permute-start | bytes 393224 | tf_op jit(solution)/shard_map/ppermute | solution.py:25
  72.4 3.4 %collective-permute-start.8 = (bf16[8,64,128]{2,1,0:T(8,128)(2,1)S(1)}, bf16[8,64,128]{2,1,0:T(8,128)(2,1)S(1)}, u32[]{:S(2)}, u32[]{:S(2)}) collective-permute-start(bf16[8,64,128]{2,1,0:T(8,128)(2,1)S(1)} %get-tuple-element.38.mine), channel_id=1, source_target_pairs={{0,1},{1,0},{2,3},{3,2},{4,5},{5,4},{6,7},{7,6},{8,9},{9,8},{10,11... | collective-permute-start | bytes 393224 | tf_op jit(solution)/shard_map/ppermute | solution.py:25
  75.8 1.3 collective-permute-done.5.theirs
  77.1 0.6 copy-done.6
  77.7 1.9 %collect.2 = (bf16[8,64,128]{2,1,0:T(8,128)(2,1)}, bf16[8,64,128]{2,1,0:T(8,128)(2,1)}) custom-call(s32[16]{0:T(128)} %compare_select_fusion.9.slot, bf16[8,64,128]{2,1,0:T(8,128)(2,1)} %copy-done.2, bf16[8,64,128]{2,1,0:T(8,128)(2,1)} %copy-done.6), custom_call_target="tpu_custom_call" | custom-call | flops 131072 | bytes 524288 | tf_op jit(solution)/shard_map/collect/pallas_call | solution.py:88
  79.6 6.0 %collective-permute-start.6 = (bf16[8,64,128]{2,1,0:T(8,128)(2,1)}, bf16[8,64,128]{2,1,0:T(8,128)(2,1)S(1)}, u32[]{:S(2)}, u32[]{:S(2)}) collective-permute-start(bf16[8,64,128]{2,1,0:T(8,128)(2,1)} %get-tuple-element.37), channel_id=1, source_target_pairs={{0,2},{1,3},{2,0},{3,1},{4,6},{5,7},{6,4},{7,5},{8,10},{9,11},{10,... | collective-permute-start | bytes 393224 | tf_op jit(solution)/shard_map/ppermute | solution.py:25
  86.3 1.9 %collect.3 = (bf16[8,64,128]{2,1,0:T(8,128)(2,1)}, bf16[8,64,128]{2,1,0:T(8,128)(2,1)}) custom-call(s32[16]{0:T(128)} %compare_select_fusion.9.slot, bf16[8,64,128]{2,1,0:T(8,128)(2,1)} %copy-done.1, bf16[8,64,128]{2,1,0:T(8,128)(2,1)} %copy-done.7), custom_call_target="tpu_custom_call" | custom-call | flops 131072 | bytes 524288 | tf_op jit(solution)/shard_map/collect/pallas_call | solution.py:88
  88.2 1.9 %collective-permute-start.9 = (bf16[8,64,128]{2,1,0:T(8,128)(2,1)}, bf16[8,64,128]{2,1,0:T(8,128)(2,1)S(1)}, u32[]{:S(2)}, u32[]{:S(2)}) collective-permute-start(bf16[8,64,128]{2,1,0:T(8,128)(2,1)} %get-tuple-element.40), channel_id=1, source_target_pairs={{0,2},{1,3},{2,0},{3,1},{4,6},{5,7},{6,4},{7,5},{8,10},{9,11},{10,... | collective-permute-start | bytes 393224 | tf_op jit(solution)/shard_map/ppermute | solution.py:25
  90.2 2.3 %collective-permute-done.6 = bf16[8,64,128]{2,1,0:T(8,128)(2,1)S(1)} collective-permute-done((bf16[8,64,128]{2,1,0:T(8,128)(2,1)}, bf16[8,64,128]{2,1,0:T(8,128)(2,1)S(1)}, u32[]{:S(2)}, u32[]{:S(2)}) %collective-permute-start.6) | collective-permute-done | bytes 131104 | tf_op jit(solution)/shard_map/ppermute | solution.py:25
  92.6 5.2 %collective-permute-start.7 = (bf16[4,64,128]{2,1,0:T(8,128)(2,1)S(1)}, bf16[4,64,128]{2,1,0:T(8,128)(2,1)S(1)}, u32[]{:S(2)}, u32[]{:S(2)}) collective-permute-start(bf16[4,64,128]{2,1,0:T(8,128)(2,1)S(1)} %get-tuple-element.44), channel_id=1, source_target_pairs={{0,4},{1,5},{2,6},{3,7},{4,0},{5,1},{6,2},{7,3},{8,12},{9,13},{10,... | collective-permute-start | bytes 196616 | tf_op jit(solution)/shard_map/ppermute | solution.py:25
  97.8 2.1 %collective-permute-done.9 = bf16[8,64,128]{2,1,0:T(8,128)(2,1)S(1)} collective-permute-done((bf16[8,64,128]{2,1,0:T(8,128)(2,1)}, bf16[8,64,128]{2,1,0:T(8,128)(2,1)S(1)}, u32[]{:S(2)}, u32[]{:S(2)}) %collective-permute-start.9) | collective-permute-done | bytes 131104 | tf_op jit(solution)/shard_map/ppermute | solution.py:25
  99.9 5.1 %collective-permute-start.10 = (bf16[4,64,128]{2,1,0:T(8,128)(2,1)S(1)}, bf16[4,64,128]{2,1,0:T(8,128)(2,1)S(1)}, u32[]{:S(2)}, u32[]{:S(2)}) collective-permute-start(bf16[4,64,128]{2,1,0:T(8,128)(2,1)S(1)} %get-tuple-element.46), channel_id=1, source_target_pairs={{0,4},{1,5},{2,6},{3,7},{4,0},{5,1},{6,2},{7,3},{8,12},{9,13},{10,... | collective-permute-start | bytes 196616 | tf_op jit(solution)/shard_map/ppermute | solution.py:25
  105.1 6.4 %collective-permute-done.10 = bf16[4,64,128]{2,1,0:T(8,128)(2,1)S(1)} collective-permute-done((bf16[4,64,128]{2,1,0:T(8,128)(2,1)S(1)}, bf16[4,64,128]{2,1,0:T(8,128)(2,1)S(1)}, u32[]{:S(2)}, u32[]{:S(2)}) %collective-permute-start.10) | collective-permute-done | bytes 65568 | tf_op jit(solution)/shard_map/ppermute | solution.py:25
  111.5 17.7 %collective-permute-start.11 = (bf16[2,128,128]{2,1,0:T(8,128)(2,1)S(1)}, bf16[2,128,128]{2,1,0:T(8,128)(2,1)S(1)}, u32[]{:S(2)}, u32[]{:S(2)}) collective-permute-start(bf16[2,128,128]{2,1,0:T(8,128)(2,1)S(1)} %pad_maximum_fusion), channel_id=1, source_target_pairs={{0,8},{1,9},{2,10},{3,11},{4,12},{5,13},{6,14},{7,15},{8,0},{9,1},... | collective-permute-start | bytes 196616 | tf_op jit(solution)/shard_map/ppermute | solution.py:25
  129.2 7.8 %collective-permute-done.11 = bf16[2,128,128]{2,1,0:T(8,128)(2,1)S(1)} collective-permute-done((bf16[2,128,128]{2,1,0:T(8,128)(2,1)S(1)}, bf16[2,128,128]{2,1,0:T(8,128)(2,1)S(1)}, u32[]{:S(2)}, u32[]{:S(2)}) %collective-permute-start.11) | collective-permute-done | bytes 65568 | tf_op jit(solution)/shard_map/ppermute | solution.py:25
  137.7 0.9 select_convert_fusion
  (43 shorter events, 2.9 us)
Async XLA Ops:
  0.0 33.7 %collective-permute-start = (bf16[256,128]{1,0:T(8,128)(2,1)}, bf16[256,128]{1,0:T(8,128)(2,1)S(1)}, u32[]{:S(2)}, u32[]{:S(2)}) collective-permute-start(bf16[256,128]{1,0:T(8,128)(2,1)} %param.10), channel_id=1, source_target_pairs={{512,0},{513,1},{514,2},{515,3},{516,4},{517,5},{518,6},{519,7},{5... | collective-permute-start | bytes 196616 | tf_op jit(solution)/shard_map/ppermute | solution.py:117
  3.3 20.5 %copy-start.3 = (bf16[256,128]{1,0:T(8,128)(2,1)S(1)}, bf16[256,128]{1,0:T(8,128)(2,1)}, u32[]{:S(2)}) copy-start(bf16[256,128]{1,0:T(8,128)(2,1)} %param.10) | copy-start | bytes 196612
  23.8 13.1 %collective-permute-start.1 = (bf16[256,128]{1,0:T(8,128)(2,1)S(1)}, bf16[256,128]{1,0:T(8,128)(2,1)S(1)}, u32[]{:S(2)}, u32[]{:S(2)}) collective-permute-start(bf16[256,128]{1,0:T(8,128)(2,1)S(1)} %copy-done.3), channel_id=1, source_target_pairs={{0,512},{1,513},{2,514},{3,515},{4,516},{5,517},{6,518},{7,519},{8... | collective-permute-start | bytes 196616 | tf_op jit(solution)/shard_map/ppermute | solution.py:120
  38.1 30.6 %copy-start = (bf16[8,1,128,128]{3,2,1,0:T(8,128)(2,1)S(1)}, bf16[8,1,128,128]{3,2,1,0:T(8,128)(2,1)}, u32[]{:S(2)}) copy-start(bf16[8,1,128,128]{3,2,1,0:T(8,128)(2,1)} %param.11) | copy-start | bytes 786436
  38.1 23.3 %all-to-all-start.2 = ((bf16[16,256,128]{2,1,0:T(8,128)(2,1)}), bf16[16,256,128]{2,1,0:T(8,128)(2,1)S(1)}, u32[]{:S(2)}, u32[]{:S(2)}) async-start(bf16[16,256,128]{2,1,0:T(8,128)(2,1)} %broadcast_in_dim.42), calls=%async_computation.2 | async-start | bytes 2097152 | tf_op jit(solution)/shard_map/all_to_all | solution.py:33
  46.3 0.7 copy-start.9
  47.0 7.5 %collective-permute-start.2 = (s32[8]{0:T(128)S(1)}, s32[8]{0:T(128)S(1)}, u32[]{:S(2)}, u32[]{:S(2)}) collective-permute-start(s32[8]{0:T(128)S(1)} %bitcast.57), channel_id=1, source_target_pairs={{0,1},{1,0},{2,3},{3,2},{4,5},{5,4},{6,7},{7,6},{8,9},{9,8},{10,11... | collective-permute-start | bytes 104 | tf_op jit(solution)/shard_map/ppermute | solution.py:25
  48.9 17.6 %collective-permute-start.3 = (bf16[4096,128]{1,0:T(8,128)(2,1)}, bf16[4096,128]{1,0:T(8,128)(2,1)S(1)}, u32[]{:S(2)}, u32[]{:S(2)}) collective-permute-start(bf16[4096,128]{1,0:T(8,128)(2,1)} %bitcast.4.s00), channel_id=1, source_target_pairs={{0,16},{16,0},{1,17},{17,1},{2,18},{18,2},{3,19},{19,3},{4,20},{20... | collective-permute-start | bytes 3145736 | tf_op jit(solution)/shard_map/ppermute | solution.py:21
  53.6 0.7 copy-start.8
  61.4 7.3 %collective-permute-start.4 = (bf16[4096,128]{1,0:T(8,128)(2,1)S(1)}, bf16[4096,128]{1,0:T(8,128)(2,1)S(1)}, u32[]{:S(2)}, u32[]{:S(2)}) collective-permute-start(bf16[4096,128]{1,0:T(8,128)(2,1)S(1)} %bitcast.46), channel_id=1, source_target_pairs={{0,16},{16,0},{1,17},{17,1},{2,18},{18,2},{3,19},{19,3},{4,20},{20... | collective-permute-start | bytes 3145736 | tf_op jit(solution)/shard_map/ppermute | solution.py:21
  70.4 6.6 %copy-start.2 = (bf16[8,64,128]{2,1,0:T(8,128)(2,1)}, bf16[8,64,128]{2,1,0:T(8,128)(2,1)S(1)}, u32[]{:S(2)}) copy-start(bf16[8,64,128]{2,1,0:T(8,128)(2,1)S(1)} %get-tuple-element.35.mine) | copy-start | bytes 393220
  70.4 9.1 %copy-start.1 = (bf16[8,64,128]{2,1,0:T(8,128)(2,1)}, bf16[8,64,128]{2,1,0:T(8,128)(2,1)S(1)}, u32[]{:S(2)}) copy-start(bf16[8,64,128]{2,1,0:T(8,128)(2,1)S(1)} %get-tuple-element.38.mine) | copy-start | bytes 393220
  70.5 6.6 %collective-permute-start.5 = (bf16[8,64,128]{2,1,0:T(8,128)(2,1)S(1)}, bf16[8,64,128]{2,1,0:T(8,128)(2,1)S(1)}, u32[]{:S(2)}, u32[]{:S(2)}) collective-permute-start(bf16[8,64,128]{2,1,0:T(8,128)(2,1)S(1)} %get-tuple-element.35.mine), channel_id=1, source_target_pairs={{0,1},{1,0},{2,3},{3,2},{4,5},{5,4},{6,7},{7,6},{8,9},{9,8},{10,11... | collective-permute-start | bytes 393224 | tf_op jit(solution)/shard_map/ppermute | solution.py:25
  72.4 13.3 %collective-permute-start.8 = (bf16[8,64,128]{2,1,0:T(8,128)(2,1)S(1)}, bf16[8,64,128]{2,1,0:T(8,128)(2,1)S(1)}, u32[]{:S(2)}, u32[]{:S(2)}) collective-permute-start(bf16[8,64,128]{2,1,0:T(8,128)(2,1)S(1)} %get-tuple-element.38.mine), channel_id=1, source_target_pairs={{0,1},{1,0},{2,3},{3,2},{4,5},{5,4},{6,7},{7,6},{8,9},{9,8},{10,11... | collective-permute-start | bytes 393224 | tf_op jit(solution)/shard_map/ppermute | solution.py:25
  77.1 0.6 copy-start.6
  79.6 6.1 %copy-start.10 = (s32[8]{0:T(128)S(1)}, s32[8]{0:T(128)}, u32[]{:S(2)}) copy-start(s32[8]{0:T(128)} %param.14) | copy-start | bytes 100
  79.6 13.0 %collective-permute-start.6 = (bf16[8,64,128]{2,1,0:T(8,128)(2,1)}, bf16[8,64,128]{2,1,0:T(8,128)(2,1)S(1)}, u32[]{:S(2)}, u32[]{:S(2)}) collective-permute-start(bf16[8,64,128]{2,1,0:T(8,128)(2,1)} %get-tuple-element.37), channel_id=1, source_target_pairs={{0,2},{1,3},{2,0},{3,1},{4,6},{5,7},{6,4},{7,5},{8,10},{9,11},{10,... | collective-permute-start | bytes 393224 | tf_op jit(solution)/shard_map/ppermute | solution.py:25
  85.7 6.9 %copy-start.4 = (bf16[8,64,128]{2,1,0:T(8,128)(2,1)S(1)}, bf16[8,64,128]{2,1,0:T(8,128)(2,1)}, u32[]{:S(2)}) copy-start(bf16[8,64,128]{2,1,0:T(8,128)(2,1)} %get-tuple-element.36) | copy-start | bytes 393220
  85.7 0.7 copy-start.7
  88.2 11.7 %collective-permute-start.9 = (bf16[8,64,128]{2,1,0:T(8,128)(2,1)}, bf16[8,64,128]{2,1,0:T(8,128)(2,1)S(1)}, u32[]{:S(2)}, u32[]{:S(2)}) collective-permute-start(bf16[8,64,128]{2,1,0:T(8,128)(2,1)} %get-tuple-element.40), channel_id=1, source_target_pairs={{0,2},{1,3},{2,0},{3,1},{4,6},{5,7},{6,4},{7,5},{8,10},{9,11},{10,... | collective-permute-start | bytes 393224 | tf_op jit(solution)/shard_map/ppermute | solution.py:25
  92.6 7.3 %copy-start.5 = (bf16[8,64,128]{2,1,0:T(8,128)(2,1)S(1)}, bf16[8,64,128]{2,1,0:T(8,128)(2,1)}, u32[]{:S(2)}) copy-start(bf16[8,64,128]{2,1,0:T(8,128)(2,1)} %get-tuple-element.39) | copy-start | bytes 393220
  92.6 12.5 %collective-permute-start.7 = (bf16[4,64,128]{2,1,0:T(8,128)(2,1)S(1)}, bf16[4,64,128]{2,1,0:T(8,128)(2,1)S(1)}, u32[]{:S(2)}, u32[]{:S(2)}) collective-permute-start(bf16[4,64,128]{2,1,0:T(8,128)(2,1)S(1)} %get-tuple-element.44), channel_id=1, source_target_pairs={{0,4},{1,5},{2,6},{3,7},{4,0},{5,1},{6,2},{7,3},{8,12},{9,13},{10,... | collective-permute-start | bytes 196616 | tf_op jit(solution)/shard_map/ppermute | solution.py:25
  99.9 11.6 %collective-permute-start.10 = (bf16[4,64,128]{2,1,0:T(8,128)(2,1)S(1)}, bf16[4,64,128]{2,1,0:T(8,128)(2,1)S(1)}, u32[]{:S(2)}, u32[]{:S(2)}) collective-permute-start(bf16[4,64,128]{2,1,0:T(8,128)(2,1)S(1)} %get-tuple-element.46), channel_id=1, source_target_pairs={{0,4},{1,5},{2,6},{3,7},{4,0},{5,1},{6,2},{7,3},{8,12},{9,13},{10,... | collective-permute-start | bytes 196616 | tf_op jit(solution)/shard_map/ppermute | solution.py:25
  111.5 25.5 %collective-permute-start.11 = (bf16[2,128,128]{2,1,0:T(8,128)(2,1)S(1)}, bf16[2,128,128]{2,1,0:T(8,128)(2,1)S(1)}, u32[]{:S(2)}, u32[]{:S(2)}) collective-permute-start(bf16[2,128,128]{2,1,0:T(8,128)(2,1)S(1)} %pad_maximum_fusion), channel_id=1, source_target_pairs={{0,8},{1,9},{2,10},{3,11},{4,12},{5,13},{6,14},{7,15},{8,0},{9,1},... | collective-permute-start | bytes 196616 | tf_op jit(solution)/shard_map/ppermute | solution.py:25
  137.1 0.7 copy-start.11

commit v3 on v2

v3 whole, which is shorter than its diff:
```python
import functools

import jax
import jax.numpy as jnp
from jax import lax
from jax.experimental import pallas as pl
from jax.experimental.pallas import tpu as pltpu
from jax.sharding import Mesh, PartitionSpec as P

WIDE = ("zh", "x", "y", "c")
PLANE = ("x", "y")
HALF, SIDE, LINE = 2, 4, 16
N_PLANE = SIDE * SIDE
SMEM = pl.BlockSpec(memory_space=pltpu.SMEM)
VMEM = pl.BlockSpec(memory_space=pltpu.VMEM)


def cost(flops, nbytes):
    return pl.CostEstimate(flops=flops, bytes_accessed=nbytes, transcendentals=0)


def swap(value, axis):
    return lax.ppermute(value, axis, [(0, 1), (1, 0)])


def exchange(value, step):
    return lax.ppermute(value, "zl", [(i, i ^ step) for i in range(LINE)])


def spread(value):
    return jnp.broadcast_to(value[None], (N_PLANE,) + value.shape)


def plane_exchange(value):
    return lax.all_to_all(value, PLANE, 0, 0)


def blank_kernel(out):
    pass


def blank(like):
    return pl.pallas_call(
        blank_kernel,
        out_shape=jax.ShapeDtypeStruct((N_PLANE,) + like.shape, like.dtype),
        out_specs=pl.BlockSpec(memory_space=pl.ANY),
        cost_estimate=cost(0, 0),
        name="blank",
    )()


def small(limit):
    return pltpu.CompilerParams(vmem_limit_bytes=limit * 2**20)


def product_kernel(facts, values, s00, s01, s10, s11, first, second, picked):
    count, width = values.shape[:2]
    half = width // 2
    shift = (s00.shape[0] // width // N_PLANE).bit_length() - 1
    zh, mine = lax.axis_index("zh"), lax.axis_index("c")
    for k in range(count):
        col = facts[count + k]
        device, inner = col >> shift, col & ((1 << shift) - 1)
        core, flat, far = device & 1, (device >> 1) & (N_PLANE - 1), (device >> 1) >> 4
        code = 2 * (far ^ zh) + (core ^ mine)
        start = pl.multiple_of(((flat << shift) + inner) * width, width)
        for number, source in enumerate((s00, s01, s10, s11)):

            @pl.when(code == number)
            def _():
                picked[k] = source[pl.ds(start, width), :]

    for k in range(count):
        out = jnp.dot(values[k], picked[k], preferred_element_type=jnp.float32)
        first[k] = out[:half].astype(first.dtype)
        second[k] = out[half:].astype(second.dtype)


def products(facts, values, sources):
    count, width, _ = values.shape
    labels = sources[0].shape[-1]
    part = jax.ShapeDtypeStruct((count, width // 2, labels), jnp.bfloat16)
    return pl.pallas_call(
        product_kernel,
        out_shape=(part, part),
        in_specs=[SMEM] + [VMEM] * 5,
        out_specs=(VMEM, VMEM),
        scratch_shapes=[pltpu.VMEM((count, width, labels), jnp.bfloat16)],
        compiler_params=small(16),
        cost_estimate=cost(2 * count * width * width * labels, 6 * count * width * labels),
        name="products",
    )(facts, values, *sources)


def collect_kernel(per_dev, order, rows, other_rows, mine, theirs, keep, send, total):
    slots = keep.shape[0]
    line = lax.axis_index("zl")
    shift = per_dev.bit_length() - 1
    total[...] = jnp.zeros_like(total)
    for numbers, source in ((rows, mine), (other_rows, theirs)):
        for k in range(source.shape[0]):
            owner, inner = numbers[k] >> shift, numbers[k] & (per_dev - 1)
            pair = ((owner >> 2) & 1) * 2 + (owner >> 3)
            differs = owner ^ line
            goes = (differs >> order[1]) & 1
            place = (pair << shift) + inner + goes * slots

            @pl.when(((differs >> order[0]) & 1) == 0)
            def _():
                total[place] += source[k].astype(jnp.float32)

    send[...] = total[slots:].astype(send.dtype)
    keep[...] = total[:slots].astype(keep.dtype)


def collect(per_dev, order, rows, other_rows, mine, theirs):
    count, height, labels = mine.shape
    slots = LINE // 4 * per_dev
    part = jax.ShapeDtypeStruct((slots, height, labels), jnp.bfloat16)
    return pl.pallas_call(
        functools.partial(collect_kernel, per_dev, order),
        out_shape=(part, part),
        in_specs=[SMEM, SMEM, VMEM, VMEM],
        out_specs=(VMEM, VMEM),
        scratch_shapes=[pltpu.VMEM((2 * slots, height, labels), jnp.float32)],
        compiler_params=small(4),
        cost_estimate=cost(2 * count * height * labels, (4 * count + 4 * slots) * height * labels),
        name="collect",
    )(rows, other_rows, mine, theirs)


def finish_kernel(anchor, first, second, came, state, out, result):
    docs, labels = state.shape
    slots, half = first.shape[:2]
    lane = lax.broadcasted_iota(jnp.int32, (1, labels), 1)
    for slot in range(slots):
        for side, keep in enumerate((first, second)):
            rows = pl.ds(side * half, half)
            here = pl.ds((slot * 2 + side) * half, half)
            total = keep[slot].astype(jnp.float32) + came[slot, rows].astype(jnp.float32)
            total = total + state[here].astype(jnp.float32)
            result[here] = total / jnp.sum(total, axis=-1, keepdims=True)
    count = anchor.shape[0] // 2
    first_row = lax.axis_index(WIDE + ("zl",)) * docs
    for k in range(count):
        row = anchor[k] - first_row
        result[pl.ds(row, 1)] = (lane == anchor[count + k]).astype(jnp.float32)
    out[...] = result[...].astype(out.dtype)


def finish(anchor, keep, came, state):
    docs, labels = state.shape
    return pl.pallas_call(
        finish_kernel,
        out_shape=jax.ShapeDtypeStruct(state.shape, state.dtype),
        in_specs=[SMEM] + [VMEM] * 4,
        out_specs=VMEM,
        scratch_shapes=[pltpu.VMEM((docs, labels), jnp.float32)],
        compiler_params=small(4),
        cost_estimate=cost(6 * docs * labels, 10 * docs * labels),
        name="finish",
    )(anchor, *keep, came, state)


def local(state, block_values, block_rows, block_cols, anchor_ids, anchor_class):
    doc_dev, labels = state.shape
    width = block_values.shape[2]
    per_dev = doc_dev // width
    values = block_values[:, 0]
    cols = block_cols[:, 0]
    rows = block_rows[:, 0]
    zh, line = lax.axis_index("zh"), lax.axis_index("zl")
    bits = {s: (line >> b) & 1 for b, s in enumerate((1, 2, 4, 8))}

    from_second = lax.ppermute(state, "zh", [(1, 0)])

    def fill(index, buffer, value):
        def gather(buffer, value):
            return plane_exchange(spread(value))

        return lax.cond(zh == index, gather, lambda buffer, value: buffer, buffer, value)

    near_own = fill(0, blank(state), state)
    again, near_own = lax.optimization_barrier((state, near_own))
    from_first = lax.ppermute(again, "zh", [(0, 1)])
    near_own, from_second = lax.optimization_barrier((near_own, from_second))
    near_own = fill(1, near_own, state)
    far = jnp.where(zh == 0, from_second, from_first)
    facts, near_own = lax.optimization_barrier((jnp.concatenate([rows, cols]), near_own))
    other_facts = tuple(exchange(facts, step) for step in (1, 2))
    far_own = plane_exchange(spread(far)).reshape(-1, labels)
    far_own, other_facts = lax.optimization_barrier((far_own, other_facts))
    near_own = near_own.reshape(-1, labels)
    near_other = swap(near_own, "c")
    far_other = swap(far_own, "c")
    mine = products(facts, values, (near_own, near_other, far_own, far_other))

    theirs = [exchange(part, step) for part, step in zip(mine, (1, 2))]
    held = [
        collect(per_dev, order, facts, *parts)
        for order, *parts in zip(((0, 1), (1, 0)), other_facts, mine, theirs)
    ]
    got = [exchange(send, step) for (_, send), step in zip(held, (2, 1))]

    def halve(keep, came, step):
        pair = (2, keep.shape[0] // 2) + keep.shape[1:]
        keep, came = keep.reshape(pair), came.reshape(pair)
        bit = bits[step]

        def at(value, index):
            starts, sizes = (index,) + (0,) * 3, (1,) + value.shape[1:]
            return lax.dynamic_slice(value, starts, sizes, allow_negative_indices=False)[0]

        def side(index):
            one = at(keep, index)
            two = at(came, index)
            return one + two

        return side(bit), side(1 - bit)

    held = [halve(keep, came, 4) for (keep, _), came in zip(held, got)]
    got = [exchange(send, 4) for _, send in held]
    held = [halve(keep, came, 8) for (keep, _), came in zip(held, got)]
    send = jnp.concatenate([send for _, send in held], axis=1)
    anchor = lax.optimization_barrier(jnp.concatenate([anchor_ids, anchor_class]))
    return finish(anchor, [keep for keep, _ in held], exchange(send, 8), state)


def solution(mesh):
    shape = (HALF, SIDE, SIDE, 2, LINE)
    every = WIDE + ("zl",)
    fine = Mesh(mesh.devices.reshape(shape), every)
    in_specs = (
        P(every, None),
        P(WIDE, "zl", None, None),
        P(WIDE, "zl"),
        P(WIDE, "zl"),
        P(every),
        P(every),
    )
    return jax.shard_map(
        local, mesh=fine, in_specs=in_specs, out_specs=P(every, None), check_vma=False
    )
```

time: 139 us -> 128 us (0.921)
  starting transfers between devices: 72.2 us -> 57.4 us
  waiting for transfers between devices: 31.8 us -> 44 us
  local copies, waits for them, and re-layouts: 7.62 us -> 2.88 us
  Pallas kernels: 5.45 us -> 3.86 us
    ppermute x8 -> x9, starting transfers between devices: 43.2 us -> 26.3 us  [exchange(): return lax.ppermute(value, 'zl', [(i, i ^ step) for i in range(LINE)])]
    ppermute x8 -> x9, waiting for transfers between devices: 19.9 us -> 31.9 us  [exchange(): return lax.ppermute(value, 'zl', [(i, i ^ step) for i in range(LINE)])]
    ppermute x1, waiting for transfers between devices: 3.19 us -> 5.21 us  [local(): from_first = lax.ppermute(again, 'zh', [(0, 1)])]
    broadcast_in_dim x2, local copies, waits for them, and re-layouts: 3.2 us -> 1.39 us  [spread(): return jnp.broadcast_to(value[None], (N_PLANE,) + value.shape)]
    all_to_all x1, waiting for transfers between devices: 6.4 us -> 4.59 us  [plane_exchange(): return lax.all_to_all(value, PLANE, 0, 0)]
    ppermute x2, starting transfers between devices: 9.72 us -> 11.4 us  [swap(): return lax.ppermute(value, axis, [(0, 1), (1, 0)])]
    unnamed x24 -> x12, local copies, waits for them, and re-layouts: 3.16 us -> 1.49 us
    pallas_call x2 -> x4, Pallas kernels: 3.73 us -> 2.88 us  [the longest x2 1.58 us: collect(): pl.pallas_call(functools.partial(collect_kernel, per_dev, order), out_sha...]
  transfers between devices with their start and end apart: 13 -> 14, of which waited for: 8 -> 9; matrix products, arithmetic and copies ran while one was open for 3% -> 0% of each run, Pallas kernels for 3% -> 1%
where the time goes in v3:
time: 128 us
  starting transfers between devices  57.4 us (45%)
  waiting for transfers between devices  44 us (34%)
  blocking collectives  19.1 us (15%)
  Pallas kernels  3.86 us (3%)
  local copies, waits for them, and re-layouts  2.88 us (2%)
    ppermute x9, waiting for transfers between devices, exchange(): return lax.ppermute(value, 'zl', [(i, i ^ step) for i in range(LINE)])  31.9 us
    ppermute x9, starting transfers between devices, exchange(): return lax.ppermute(value, 'zl', [(i, i ^ step) for i in range(LINE)])  26.3 us
    all_to_all x1, blocking collectives, plane_exchange(): return lax.all_to_all(value, PLANE, 0, 0)  19.1 us
    ppermute x2, starting transfers between devices, swap(): return lax.ppermute(value, axis, [(0, 1), (1, 0)])  11.4 us
    ppermute x1, starting transfers between devices, local(): from_first = lax.ppermute(again, 'zh', [(0, 1)])  10.2 us
    all_to_all x1, starting transfers between devices, plane_exchange(): return lax.all_to_all(value, PLANE, 0, 0)  8.19 us
    ppermute x1, waiting for transfers between devices, local(): from_first = lax.ppermute(again, 'zh', [(0, 1)])  5.21 us
    all_to_all x1, waiting for transfers between devices, plane_exchange(): return lax.all_to_all(value, PLANE, 0, 0)  4.59 us
  transfers between devices with their start and end apart: 14, of which 9 were waited for; matrix products, arithmetic and copies ran while one was open for 0% of the time, Pallas kernels for 1%

profile of v3, /device:TPU:1, one launch (start us, length us, event | category | flops | bytes accessed | tf_op | source)
XLA Modules:
  0.0 127.8 jit_solution(9151137780462776589)
XLA Ops:
  0.0 1.3 %collective-permute-start = (bf16[256,128]{1,0:T(8,128)(2,1)}, bf16[256,128]{1,0:T(8,128)(2,1)S(1)}, u32[]{:S(2)}, u32[]{:S(2)}) collective-permute-start(bf16[256,128]{1,0:T(8,128)(2,1)} %state.1), channel_id=1, source_target_pairs={{512,0},{513,1},{514,2},{515,3},{516,4},{517,5},{518,6},{519,7},{5... | collective-permute-start | bytes 196616 | tf_op jit(solution)/shard_map/ppermute | solution.py:175
  1.3 0.8 copy-done.1
  2.1 19.3 %conditional.2 = (bf16[16,256,128]{2,1,0:T(8,128)(2,1)S(1)}) conditional(s32[]{:T(128)} %convert_element_type.7, bf16[16,256,128]{2,1,0:T(8,128)(2,1)S(1)} %blank.1, bf16[256,128]{1,0:T(8,128)(2,1)S(1)} %copy-done.1), branch_computations={%region_0.0_spmd, %region_1.0_spmd} | conditional | bytes 3211272 | solution.py:181
  2.3 19.1 %all_to_all.13 = bf16[16,256,128]{2,1,0:T(8,128)(2,1)S(1)} all-to-all(bf16[16,256,128]{2,1,0:T(8,128)(2,1)S(1)} %broadcast_in_dim.2), channel_id=1, replica_groups=mesh['zh'=2,'x'=4,'y'=4,'c'=2,'zl'=16] {'x','y'}, dimensions={0} | all-to-all | bytes 2097152 | tf_op jit(solution)/shard_map/cond/branch_1_fun/all_to_all | solution.py:35
  21.5 10.2 %collective-permute-start.1 = (bf16[256,128]{1,0:T(8,128)(2,1)S(1)}, bf16[256,128]{1,0:T(8,128)(2,1)S(1)}, u32[]{:S(2)}, u32[]{:S(2)}) collective-permute-start(bf16[256,128]{1,0:T(8,128)(2,1)S(1)} %copy-done.1), channel_id=1, source_target_pairs={{0,512},{1,513},{2,514},{3,515},{4,516},{5,517},{6,518},{7,519},{8... | collective-permute-start | bytes 196616 | tf_op jit(solution)/shard_map/ppermute | solution.py:185
  31.7 5.2 %collective-permute-done.1 = bf16[256,128]{1,0:T(8,128)(2,1)S(1)} collective-permute-done((bf16[256,128]{1,0:T(8,128)(2,1)S(1)}, bf16[256,128]{1,0:T(8,128)(2,1)S(1)}, u32[]{:S(2)}, u32[]{:S(2)}) %collective-permute-start.1) | collective-permute-done | bytes 65568 | tf_op jit(solution)/shard_map/ppermute | solution.py:185
  36.9 1.2 broadcast_in_dim.10
  38.1 8.2 %all-to-all-start.2 = ((bf16[16,256,128]{2,1,0:T(8,128)(2,1)}), bf16[16,256,128]{2,1,0:T(8,128)(2,1)S(1)}, u32[]{:S(2)}, u32[]{:S(2)}) async-start(bf16[16,256,128]{2,1,0:T(8,128)(2,1)} %broadcast_in_dim.10), calls=%async_computation.2 | async-start | bytes 2097152 | tf_op jit(solution)/shard_map/all_to_all | solution.py:35
  46.3 0.6 copy-done.2
  47.1 1.9 %collective-permute-start.2 = (s32[16]{0:T(128)S(1)}, s32[16]{0:T(128)S(1)}, u32[]{:S(2)}, u32[]{:S(2)}) collective-permute-start(s32[16]{0:T(128)S(1)} %pad_add_fusion.1.facts.rows), channel_id=1, source_target_pairs={{0,1},{1,0},{2,3},{3,2},{4,5},{5,4},{6,7},{7,6},{8,9},{9,8},{10,11... | collective-permute-start | bytes 200 | tf_op jit(solution)/shard_map/ppermute | solution.py:27
  49.0 1.9 %collective-permute-start.3 = (s32[16]{0:T(128)S(1)}, s32[16]{0:T(128)S(1)}, u32[]{:S(2)}, u32[]{:S(2)}) collective-permute-start(s32[16]{0:T(128)S(1)} %pad_add_fusion.1.facts.rows), channel_id=1, source_target_pairs={{0,2},{1,3},{2,0},{3,1},{4,6},{5,7},{6,4},{7,5},{8,10},{9,11},{10,... | collective-permute-start | bytes 200 | tf_op jit(solution)/shard_map/ppermute | solution.py:27
  50.9 6.0 %collective-permute-start.4 = (bf16[4096,128]{1,0:T(8,128)(2,1)S(1)}, bf16[4096,128]{1,0:T(8,128)(2,1)S(1)}, u32[]{:S(2)}, u32[]{:S(2)}) collective-permute-start(bf16[4096,128]{1,0:T(8,128)(2,1)S(1)} %bitcast.30), channel_id=1, source_target_pairs={{0,16},{16,0},{1,17},{17,1},{2,18},{18,2},{3,19},{19,3},{4,20},{20... | collective-permute-start | bytes 3145736 | tf_op jit(solution)/shard_map/ppermute | solution.py:23
  56.9 4.6 %all-to-all-done.2 = bf16[16,256,128]{2,1,0:T(8,128)(2,1)S(1)} async-done(((bf16[16,256,128]{2,1,0:T(8,128)(2,1)}), bf16[16,256,128]{2,1,0:T(8,128)(2,1)S(1)}, u32[]{:S(2)}, u32[]{:S(2)}) %all-to-all-start.2) | async-done | bytes 1048608 | tf_op jit(solution)/shard_map/all_to_all | solution.py:35
  61.5 5.4 %collective-permute-start.5 = (bf16[4096,128]{1,0:T(8,128)(2,1)S(1)}, bf16[4096,128]{1,0:T(8,128)(2,1)S(1)}, u32[]{:S(2)}, u32[]{:S(2)}) collective-permute-start(bf16[4096,128]{1,0:T(8,128)(2,1)S(1)} %bitcast.25), channel_id=1, source_target_pairs={{0,16},{16,0},{1,17},{17,1},{2,18},{18,2},{3,19},{19,3},{4,20},{20... | collective-permute-start | bytes 3145736 | tf_op jit(solution)/shard_map/ppermute | solution.py:23
  67.0 2.3 %collective-permute-done.5.s11 = bf16[4096,128]{1,0:T(8,128)(2,1)S(1)} collective-permute-done((bf16[4096,128]{1,0:T(8,128)(2,1)S(1)}, bf16[4096,128]{1,0:T(8,128)(2,1)S(1)}, u32[]{:S(2)}, u32[]{:S(2)}) %collective-permute-start.5) | collective-permute-done | bytes 1048608 | tf_op jit(solution)/shard_map/ppermute | solution.py:23
  69.2 1.0 products.1
  70.2 1.9 %collective-permute-start.9 = (bf16[8,64,128]{2,1,0:T(8,128)(2,1)S(1)}, bf16[8,64,128]{2,1,0:T(8,128)(2,1)S(1)}, u32[]{:S(2)}, u32[]{:S(2)}) collective-permute-start(bf16[8,64,128]{2,1,0:T(8,128)(2,1)S(1)} %get-tuple-element.42.mine), channel_id=1, source_target_pairs={{0,2},{1,3},{2,0},{3,1},{4,6},{5,7},{6,4},{7,5},{8,10},{9,11},{10,... | collective-permute-start | bytes 393224 | tf_op jit(solution)/shard_map/ppermute | solution.py:27
  72.2 1.9 %collective-permute-start.6 = (bf16[8,64,128]{2,1,0:T(8,128)(2,1)S(1)}, bf16[8,64,128]{2,1,0:T(8,128)(2,1)S(1)}, u32[]{:S(2)}, u32[]{:S(2)}) collective-permute-start(bf16[8,64,128]{2,1,0:T(8,128)(2,1)S(1)} %get-tuple-element.38.mine), channel_id=1, source_target_pairs={{0,1},{1,0},{2,3},{3,2},{4,5},{5,4},{6,7},{7,6},{8,9},{9,8},{10,11... | collective-permute-start | bytes 393224 | tf_op jit(solution)/shard_map/ppermute | solution.py:27
  74.1 3.6 %collective-permute-done.9.theirs = bf16[8,64,128]{2,1,0:T(8,128)(2,1)S(1)} collective-permute-done((bf16[8,64,128]{2,1,0:T(8,128)(2,1)S(1)}, bf16[8,64,128]{2,1,0:T(8,128)(2,1)S(1)}, u32[]{:S(2)}, u32[]{:S(2)}) %collective-permute-start.9) | collective-permute-done | bytes 131104 | tf_op jit(solution)/shard_map/ppermute | solution.py:27
  77.7 0.8 collect.3
  78.5 1.9 %collective-permute-start.10 = (bf16[8,64,128]{2,1,0:T(8,128)(2,1)S(1)}, bf16[8,64,128]{2,1,0:T(8,128)(2,1)S(1)}, u32[]{:S(2)}, u32[]{:S(2)}) collective-permute-start(bf16[8,64,128]{2,1,0:T(8,128)(2,1)S(1)} %get-tuple-element.44), channel_id=1, source_target_pairs={{0,1},{1,0},{2,3},{3,2},{4,5},{5,4},{6,7},{7,6},{8,9},{9,8},{10,11... | collective-permute-start | bytes 393224 | tf_op jit(solution)/shard_map/ppermute | solution.py:27
  80.5 0.8 collective-permute-done.6.theirs
  81.3 0.8 collect.2
  82.1 1.9 %collective-permute-start.7 = (bf16[8,64,128]{2,1,0:T(8,128)(2,1)S(1)}, bf16[8,64,128]{2,1,0:T(8,128)(2,1)S(1)}, u32[]{:S(2)}, u32[]{:S(2)}) collective-permute-start(bf16[8,64,128]{2,1,0:T(8,128)(2,1)S(1)} %get-tuple-element.40), channel_id=1, source_target_pairs={{0,2},{1,3},{2,0},{3,1},{4,6},{5,7},{6,4},{7,5},{8,10},{9,11},{10,... | collective-permute-start | bytes 393224 | tf_op jit(solution)/shard_map/ppermute | solution.py:27
  84.0 0.2 collective-permute-done.10
  84.3 4.9 %collective-permute-start.11 = (bf16[4,64,128]{2,1,0:T(8,128)(2,1)S(1)}, bf16[4,64,128]{2,1,0:T(8,128)(2,1)S(1)}, u32[]{:S(2)}, u32[]{:S(2)}) collective-permute-start(bf16[4,64,128]{2,1,0:T(8,128)(2,1)S(1)} %get-tuple-element.46), channel_id=1, source_target_pairs={{0,4},{1,5},{2,6},{3,7},{4,0},{5,1},{6,2},{7,3},{8,12},{9,13},{10,... | collective-permute-start | bytes 196616 | tf_op jit(solution)/shard_map/ppermute | solution.py:27
  89.2 3.5 %collective-permute-done.7 = bf16[8,64,128]{2,1,0:T(8,128)(2,1)S(1)} collective-permute-done((bf16[8,64,128]{2,1,0:T(8,128)(2,1)S(1)}, bf16[8,64,128]{2,1,0:T(8,128)(2,1)S(1)}, u32[]{:S(2)}, u32[]{:S(2)}) %collective-permute-start.7) | collective-permute-done | bytes 131104 | tf_op jit(solution)/shard_map/ppermute | solution.py:27
  92.7 1.9 %collective-permute-start.8 = (bf16[4,64,128]{2,1,0:T(8,128)(2,1)S(1)}, bf16[4,64,128]{2,1,0:T(8,128)(2,1)S(1)}, u32[]{:S(2)}, u32[]{:S(2)}) collective-permute-start(bf16[4,64,128]{2,1,0:T(8,128)(2,1)S(1)} %get-tuple-element.48), channel_id=1, source_target_pairs={{0,4},{1,5},{2,6},{3,7},{4,0},{5,1},{6,2},{7,3},{8,12},{9,13},{10,... | collective-permute-start | bytes 196616 | tf_op jit(solution)/shard_map/ppermute | solution.py:27
  94.7 10.1 %collective-permute-done.8 = bf16[4,64,128]{2,1,0:T(8,128)(2,1)S(1)} collective-permute-done((bf16[4,64,128]{2,1,0:T(8,128)(2,1)S(1)}, bf16[4,64,128]{2,1,0:T(8,128)(2,1)S(1)}, u32[]{:S(2)}, u32[]{:S(2)}) %collective-permute-start.8) | collective-permute-done | bytes 65568 | tf_op jit(solution)/shard_map/ppermute | solution.py:27
  104.8 7.9 %collective-permute-start.12 = (bf16[2,128,128]{2,1,0:T(8,128)(2,1)S(1)}, bf16[2,128,128]{2,1,0:T(8,128)(2,1)S(1)}, u32[]{:S(2)}, u32[]{:S(2)}) collective-permute-start(bf16[2,128,128]{2,1,0:T(8,128)(2,1)S(1)} %pad_maximum_fusion), channel_id=1, source_target_pairs={{0,8},{1,9},{2,10},{3,11},{4,12},{5,13},{6,14},{7,15},{8,0},{9,1},... | collective-permute-start | bytes 196616 | tf_op jit(solution)/shard_map/ppermute | solution.py:27
  112.9 13.7 %collective-permute-done.12.came = bf16[2,128,128]{2,1,0:T(8,128)(2,1)S(1)} collective-permute-done((bf16[2,128,128]{2,1,0:T(8,128)(2,1)S(1)}, bf16[2,128,128]{2,1,0:T(8,128)(2,1)S(1)}, u32[]{:S(2)}, u32[]{:S(2)}) %collective-permute-start.12) | collective-permute-done | bytes 65568 | tf_op jit(solution)/shard_map/ppermute | solution.py:27
  126.5 1.3 %finish.1 = bf16[256,128]{1,0:T(8,128)(2,1)} custom-call(s32[16]{0:T(128)S(1)} %pad_add_fusion.anchor, bf16[2,64,128]{2,1,0:T(8,128)(2,1)S(1)} %get-tuple-element.50.first, bf16[2,64,128]{2,1,0:T(8,128)(2,1)S(1)} %get-tuple-element.52.second, bf16[2,128,128]{2,1,0:T(8,128)(2,1)S(1)} %collective-permute-done.12.came, bf16[256,128]{1,0:T(8,128)(2,1)S(1)} %copy-done.1), custom_call_target="tpu_custom_call" | custom-call | flops 196608 | bytes 327680 | tf_op jit(solution)/shard_map/finish/pallas_call | solution.py:153
  (26 shorter events, 0.5 us)
Async XLA Ops:
  0.0 31.7 %collective-permute-start = (bf16[256,128]{1,0:T(8,128)(2,1)}, bf16[256,128]{1,0:T(8,128)(2,1)S(1)}, u32[]{:S(2)}, u32[]{:S(2)}) collective-permute-start(bf16[256,128]{1,0:T(8,128)(2,1)} %state.1), channel_id=1, source_target_pairs={{512,0},{513,1},{514,2},{515,3},{516,4},{517,5},{518,6},{519,7},{5... | collective-permute-start | bytes 196616 | tf_op jit(solution)/shard_map/ppermute | solution.py:175
  1.3 0.8 copy-start.1
  21.5 15.4 %collective-permute-start.1 = (bf16[256,128]{1,0:T(8,128)(2,1)S(1)}, bf16[256,128]{1,0:T(8,128)(2,1)S(1)}, u32[]{:S(2)}, u32[]{:S(2)}) collective-permute-start(bf16[256,128]{1,0:T(8,128)(2,1)S(1)} %copy-done.1), channel_id=1, source_target_pairs={{0,512},{1,513},{2,514},{3,515},{4,516},{5,517},{6,518},{7,519},{8... | collective-permute-start | bytes 196616 | tf_op jit(solution)/shard_map/ppermute | solution.py:185
  38.1 31.1 %copy-start = (bf16[8,1,128,128]{3,2,1,0:T(8,128)(2,1)S(1)}, bf16[8,1,128,128]{3,2,1,0:T(8,128)(2,1)}, u32[]{:S(2)}) copy-start(bf16[8,1,128,128]{3,2,1,0:T(8,128)(2,1)} %param.11) | copy-start | bytes 786436
  38.1 23.4 %all-to-all-start.2 = ((bf16[16,256,128]{2,1,0:T(8,128)(2,1)}), bf16[16,256,128]{2,1,0:T(8,128)(2,1)S(1)}, u32[]{:S(2)}, u32[]{:S(2)}) async-start(bf16[16,256,128]{2,1,0:T(8,128)(2,1)} %broadcast_in_dim.10), calls=%async_computation.2 | async-start | bytes 2097152 | tf_op jit(solution)/shard_map/all_to_all | solution.py:35
  46.3 0.7 copy-start.2
  46.3 0.7 copy-start.3
  47.1 9.9 %collective-permute-start.2 = (s32[16]{0:T(128)S(1)}, s32[16]{0:T(128)S(1)}, u32[]{:S(2)}, u32[]{:S(2)}) collective-permute-start(s32[16]{0:T(128)S(1)} %pad_add_fusion.1.facts.rows), channel_id=1, source_target_pairs={{0,1},{1,0},{2,3},{3,2},{4,5},{5,4},{6,7},{7,6},{8,9},{9,8},{10,11... | collective-permute-start | bytes 200 | tf_op jit(solution)/shard_map/ppermute | solution.py:27
  49.0 8.0 %collective-permute-start.3 = (s32[16]{0:T(128)S(1)}, s32[16]{0:T(128)S(1)}, u32[]{:S(2)}, u32[]{:S(2)}) collective-permute-start(s32[16]{0:T(128)S(1)} %pad_add_fusion.1.facts.rows), channel_id=1, source_target_pairs={{0,2},{1,3},{2,0},{3,1},{4,6},{5,7},{6,4},{7,5},{8,10},{9,11},{10,... | collective-permute-start | bytes 200 | tf_op jit(solution)/shard_map/ppermute | solution.py:27
  50.9 16.1 %collective-permute-start.4 = (bf16[4096,128]{1,0:T(8,128)(2,1)S(1)}, bf16[4096,128]{1,0:T(8,128)(2,1)S(1)}, u32[]{:S(2)}, u32[]{:S(2)}) collective-permute-start(bf16[4096,128]{1,0:T(8,128)(2,1)S(1)} %bitcast.30), channel_id=1, source_target_pairs={{0,16},{16,0},{1,17},{17,1},{2,18},{18,2},{3,19},{19,3},{4,20},{20... | collective-permute-start | bytes 3145736 | tf_op jit(solution)/shard_map/ppermute | solution.py:23
  61.5 7.7 %collective-permute-start.5 = (bf16[4096,128]{1,0:T(8,128)(2,1)S(1)}, bf16[4096,128]{1,0:T(8,128)(2,1)S(1)}, u32[]{:S(2)}, u32[]{:S(2)}) collective-permute-start(bf16[4096,128]{1,0:T(8,128)(2,1)S(1)} %bitcast.25), channel_id=1, source_target_pairs={{0,16},{16,0},{1,17},{17,1},{2,18},{18,2},{3,19},{19,3},{4,20},{20... | collective-permute-start | bytes 3145736 | tf_op jit(solution)/shard_map/ppermute | solution.py:23
  70.2 7.5 %collective-permute-start.9 = (bf16[8,64,128]{2,1,0:T(8,128)(2,1)S(1)}, bf16[8,64,128]{2,1,0:T(8,128)(2,1)S(1)}, u32[]{:S(2)}, u32[]{:S(2)}) collective-permute-start(bf16[8,64,128]{2,1,0:T(8,128)(2,1)S(1)} %get-tuple-element.42.mine), channel_id=1, source_target_pairs={{0,2},{1,3},{2,0},{3,1},{4,6},{5,7},{6,4},{7,5},{8,10},{9,11},{10,... | collective-permute-start | bytes 393224 | tf_op jit(solution)/shard_map/ppermute | solution.py:27
  72.2 9.1 %collective-permute-start.6 = (bf16[8,64,128]{2,1,0:T(8,128)(2,1)S(1)}, bf16[8,64,128]{2,1,0:T(8,128)(2,1)S(1)}, u32[]{:S(2)}, u32[]{:S(2)}) collective-permute-start(bf16[8,64,128]{2,1,0:T(8,128)(2,1)S(1)} %get-tuple-element.38.mine), channel_id=1, source_target_pairs={{0,1},{1,0},{2,3},{3,2},{4,5},{5,4},{6,7},{7,6},{8,9},{9,8},{10,11... | collective-permute-start | bytes 393224 | tf_op jit(solution)/shard_map/ppermute | solution.py:27
  78.5 5.7 %collective-permute-start.10 = (bf16[8,64,128]{2,1,0:T(8,128)(2,1)S(1)}, bf16[8,64,128]{2,1,0:T(8,128)(2,1)S(1)}, u32[]{:S(2)}, u32[]{:S(2)}) collective-permute-start(bf16[8,64,128]{2,1,0:T(8,128)(2,1)S(1)} %get-tuple-element.44), channel_id=1, source_target_pairs={{0,1},{1,0},{2,3},{3,2},{4,5},{5,4},{6,7},{7,6},{8,9},{9,8},{10,11... | collective-permute-start | bytes 393224 | tf_op jit(solution)/shard_map/ppermute | solution.py:27
  82.1 10.6 %collective-permute-start.7 = (bf16[8,64,128]{2,1,0:T(8,128)(2,1)S(1)}, bf16[8,64,128]{2,1,0:T(8,128)(2,1)S(1)}, u32[]{:S(2)}, u32[]{:S(2)}) collective-permute-start(bf16[8,64,128]{2,1,0:T(8,128)(2,1)S(1)} %get-tuple-element.40), channel_id=1, source_target_pairs={{0,2},{1,3},{2,0},{3,1},{4,6},{5,7},{6,4},{7,5},{8,10},{9,11},{10,... | collective-permute-start | bytes 393224 | tf_op jit(solution)/shard_map/ppermute | solution.py:27
  84.3 10.4 %collective-permute-start.11 = (bf16[4,64,128]{2,1,0:T(8,128)(2,1)S(1)}, bf16[4,64,128]{2,1,0:T(8,128)(2,1)S(1)}, u32[]{:S(2)}, u32[]{:S(2)}) collective-permute-start(bf16[4,64,128]{2,1,0:T(8,128)(2,1)S(1)} %get-tuple-element.46), channel_id=1, source_target_pairs={{0,4},{1,5},{2,6},{3,7},{4,0},{5,1},{6,2},{7,3},{8,12},{9,13},{10,... | collective-permute-start | bytes 196616 | tf_op jit(solution)/shard_map/ppermute | solution.py:27
  92.7 12.0 %collective-permute-start.8 = (bf16[4,64,128]{2,1,0:T(8,128)(2,1)S(1)}, bf16[4,64,128]{2,1,0:T(8,128)(2,1)S(1)}, u32[]{:S(2)}, u32[]{:S(2)}) collective-permute-start(bf16[4,64,128]{2,1,0:T(8,128)(2,1)S(1)} %get-tuple-element.48), channel_id=1, source_target_pairs={{0,4},{1,5},{2,6},{3,7},{4,0},{5,1},{6,2},{7,3},{8,12},{9,13},{10,... | collective-permute-start | bytes 196616 | tf_op jit(solution)/shard_map/ppermute | solution.py:27
  104.8 8.0 %copy-start.4 = (s32[8]{0:T(128)S(1)}, s32[8]{0:T(128)}, u32[]{:S(2)}) copy-start(s32[8]{0:T(128)} %param.15) | copy-start | bytes 100
  104.8 8.0 %copy-start.5 = (s32[8]{0:T(128)S(1)}, s32[8]{0:T(128)}, u32[]{:S(2)}) copy-start(s32[8]{0:T(128)} %param.14) | copy-start | bytes 100
  104.8 21.7 %collective-permute-start.12 = (bf16[2,128,128]{2,1,0:T(8,128)(2,1)S(1)}, bf16[2,128,128]{2,1,0:T(8,128)(2,1)S(1)}, u32[]{:S(2)}, u32[]{:S(2)}) collective-permute-start(bf16[2,128,128]{2,1,0:T(8,128)(2,1)S(1)} %pad_maximum_fusion), channel_id=1, source_target_pairs={{0,8},{1,9},{2,10},{3,11},{4,12},{5,13},{6,14},{7,15},{8,0},{9,1},... | collective-permute-start | bytes 196616 | tf_op jit(solution)/shard_map/ppermute | solution.py:27

commit v4 on v3

--- a/solution.py
+++ b/solution.py
@@ -129,15 +129,14 @@
     )(rows, other_rows, mine, theirs)
 
 
-def finish_kernel(anchor, first, second, came, state, out, result):
+def finish_kernel(anchor, first, second, came_first, came_second, state, out, result):
     docs, labels = state.shape
     slots, half = first.shape[:2]
     lane = lax.broadcasted_iota(jnp.int32, (1, labels), 1)
     for slot in range(slots):
-        for side, keep in enumerate((first, second)):
-            rows = pl.ds(side * half, half)
+        for side, (keep, came) in enumerate(((first, came_first), (second, came_second))):
             here = pl.ds((slot * 2 + side) * half, half)
-            total = keep[slot].astype(jnp.float32) + came[slot, rows].astype(jnp.float32)
+            total = keep[slot].astype(jnp.float32) + came[slot].astype(jnp.float32)
             total = total + state[here].astype(jnp.float32)
             result[here] = total / jnp.sum(total, axis=-1, keepdims=True)
     count = anchor.shape[0] // 2
@@ -153,13 +152,13 @@
     return pl.pallas_call(
         finish_kernel,
         out_shape=jax.ShapeDtypeStruct(state.shape, state.dtype),
-        in_specs=[SMEM] + [VMEM] * 4,
+        in_specs=[SMEM] + [VMEM] * 5,
         out_specs=VMEM,
         scratch_shapes=[pltpu.VMEM((docs, labels), jnp.float32)],
         compiler_params=small(4),
         cost_estimate=cost(6 * docs * labels, 10 * docs * labels),
         name="finish",
-    )(anchor, *keep, came, state)
+    )(anchor, *keep, *came, state)
 
 
 def local(state, block_values, block_rows, block_cols, anchor_ids, anchor_class):
@@ -221,9 +220,8 @@
     held = [halve(keep, came, 4) for (keep, _), came in zip(held, got)]
     got = [exchange(send, 4) for _, send in held]
     held = [halve(keep, came, 8) for (keep, _), came in zip(held, got)]
-    send = jnp.concatenate([send for _, send in held], axis=1)
     anchor = lax.optimization_barrier(jnp.concatenate([anchor_ids, anchor_class]))
-    return finish(anchor, [keep for keep, _ in held], exchange(send, 8), state)
+    return finish(anchor, [keep for keep, _ in held], [exchange(send, 8) for _, send in held], state)
 
 
 def solution(mesh):

time: 128 us -> 128 us (level)
  the two profiles are of different devices: /device:TPU:1 before, /device:TPU:8 now
where the time goes in v4:
time: 128 us
  starting transfers between devices  60.4 us (47%)
  waiting for transfers between devices  32.7 us (26%)
  blocking collectives  27.2 us (21%)
  Pallas kernels  3.87 us (3%)
  local copies, waits for them, and re-layouts  2.87 us (2%)
    ppermute x10, starting transfers between devices, exchange(): return lax.ppermute(value, 'zl', [(i, i ^ step) for i in range(LINE)])  46.2 us
    all_to_all x1, blocking collectives, plane_exchange(): return lax.all_to_all(value, PLANE, 0, 0)  27.2 us
    ppermute x10, waiting for transfers between devices, exchange(): return lax.ppermute(value, 'zl', [(i, i ^ step) for i in range(LINE)])  17.3 us
    all_to_all x1, starting transfers between devices, plane_exchange(): return lax.all_to_all(value, PLANE, 0, 0)  7.52 us
    all_to_all x1, waiting for transfers between devices, plane_exchange(): return lax.all_to_all(value, PLANE, 0, 0)  6.76 us
    ppermute x1, waiting for transfers between devices, local(): from_first = lax.ppermute(again, 'zh', [(0, 1)])  6.06 us
    ppermute x2, starting transfers between devices, swap(): return lax.ppermute(value, axis, [(0, 1), (1, 0)])  3.83 us
    ppermute x2, waiting for transfers between devices, swap(): return lax.ppermute(value, axis, [(0, 1), (1, 0)])  2.62 us
  transfers between devices with their start and end apart: 15, of which 7 were waited for; matrix products, arithmetic and copies ran while one was open for 0% of the time, Pallas kernels for 1%

profile of v4, /device:TPU:8, one launch (start us, length us, event | category | flops | bytes accessed | tf_op | source)
XLA Modules:
  0.0 127.6 jit_solution(16515497017017410376)
XLA Ops:
  0.0 1.3 %collective-permute-start = (bf16[256,128]{1,0:T(8,128)(2,1)}, bf16[256,128]{1,0:T(8,128)(2,1)S(1)}, u32[]{:S(2)}, u32[]{:S(2)}) collective-permute-start(bf16[256,128]{1,0:T(8,128)(2,1)} %state.1), channel_id=1, source_target_pairs={{512,0},{513,1},{514,2},{515,3},{516,4},{517,5},{518,6},{519,7},{5... | collective-permute-start | bytes 196616 | tf_op jit(solution)/shard_map/ppermute | solution.py:174
  1.3 0.8 copy-done.1
  2.1 27.4 %conditional.2 = (bf16[16,256,128]{2,1,0:T(8,128)(2,1)S(1)}) conditional(s32[]{:T(128)} %convert_element_type.7, bf16[16,256,128]{2,1,0:T(8,128)(2,1)S(1)} %blank.1, bf16[256,128]{1,0:T(8,128)(2,1)S(1)} %copy-done.1), branch_computations={%region_0.0_spmd, %region_1.0_spmd} | conditional | bytes 3211272 | solution.py:180
  2.1 0.2 broadcast_in_dim.2
  2.3 27.2 %all_to_all.13 = bf16[16,256,128]{2,1,0:T(8,128)(2,1)S(1)} all-to-all(bf16[16,256,128]{2,1,0:T(8,128)(2,1)S(1)} %broadcast_in_dim.2), channel_id=1, replica_groups=mesh['zh'=2,'x'=4,'y'=4,'c'=2,'zl'=16] {'x','y'}, dimensions={0} | all-to-all | bytes 2097152 | tf_op jit(solution)/shard_map/cond/branch_1_fun/all_to_all | solution.py:35
  29.5 1.6 %collective-permute-start.1 = (bf16[256,128]{1,0:T(8,128)(2,1)S(1)}, bf16[256,128]{1,0:T(8,128)(2,1)S(1)}, u32[]{:S(2)}, u32[]{:S(2)}) collective-permute-start(bf16[256,128]{1,0:T(8,128)(2,1)S(1)} %copy-done.1), channel_id=1, source_target_pairs={{0,512},{1,513},{2,514},{3,515},{4,516},{5,517},{6,518},{7,519},{8... | collective-permute-start | bytes 196616 | tf_op jit(solution)/shard_map/ppermute | solution.py:184
  31.1 6.1 %collective-permute-done.1 = bf16[256,128]{1,0:T(8,128)(2,1)S(1)} collective-permute-done((bf16[256,128]{1,0:T(8,128)(2,1)S(1)}, bf16[256,128]{1,0:T(8,128)(2,1)S(1)}, u32[]{:S(2)}, u32[]{:S(2)}) %collective-permute-start.1) | collective-permute-done | bytes 65568 | tf_op jit(solution)/shard_map/ppermute | solution.py:184
  37.2 1.2 broadcast_in_dim.10
  38.4 7.5 %all-to-all-start.2 = ((bf16[16,256,128]{2,1,0:T(8,128)(2,1)}), bf16[16,256,128]{2,1,0:T(8,128)(2,1)S(1)}, u32[]{:S(2)}, u32[]{:S(2)}) async-start(bf16[16,256,128]{2,1,0:T(8,128)(2,1)} %broadcast_in_dim.10), calls=%async_computation.2 | async-start | bytes 2097152 | tf_op jit(solution)/shard_map/all_to_all | solution.py:35
  45.9 0.6 copy-done.2
  46.7 1.9 %collective-permute-start.2 = (s32[16]{0:T(128)S(1)}, s32[16]{0:T(128)S(1)}, u32[]{:S(2)}, u32[]{:S(2)}) collective-permute-start(s32[16]{0:T(128)S(1)} %pad_add_fusion.1.facts.rows), channel_id=1, source_target_pairs={{0,1},{1,0},{2,3},{3,2},{4,5},{5,4},{6,7},{7,6},{8,9},{9,8},{10,11... | collective-permute-start | bytes 200 | tf_op jit(solution)/shard_map/ppermute | solution.py:27
  48.6 5.2 %collective-permute-start.3 = (s32[16]{0:T(128)S(1)}, s32[16]{0:T(128)S(1)}, u32[]{:S(2)}, u32[]{:S(2)}) collective-permute-start(s32[16]{0:T(128)S(1)} %pad_add_fusion.1.facts.rows), channel_id=1, source_target_pairs={{0,2},{1,3},{2,0},{3,1},{4,6},{5,7},{6,4},{7,5},{8,10},{9,11},{10,... | collective-permute-start | bytes 200 | tf_op jit(solution)/shard_map/ppermute | solution.py:27
  53.8 1.9 %collective-permute-start.4 = (bf16[4096,128]{1,0:T(8,128)(2,1)S(1)}, bf16[4096,128]{1,0:T(8,128)(2,1)S(1)}, u32[]{:S(2)}, u32[]{:S(2)}) collective-permute-start(bf16[4096,128]{1,0:T(8,128)(2,1)S(1)} %bitcast.30), channel_id=1, source_target_pairs={{0,16},{16,0},{1,17},{17,1},{2,18},{18,2},{3,19},{19,3},{4,20},{20... | collective-permute-start | bytes 3145736 | tf_op jit(solution)/shard_map/ppermute | solution.py:23
  55.8 6.8 %all-to-all-done.2 = bf16[16,256,128]{2,1,0:T(8,128)(2,1)S(1)} async-done(((bf16[16,256,128]{2,1,0:T(8,128)(2,1)}), bf16[16,256,128]{2,1,0:T(8,128)(2,1)S(1)}, u32[]{:S(2)}, u32[]{:S(2)}) %all-to-all-start.2) | async-done | bytes 1048608 | tf_op jit(solution)/shard_map/all_to_all | solution.py:35
  62.6 1.9 %collective-permute-start.5 = (bf16[4096,128]{1,0:T(8,128)(2,1)S(1)}, bf16[4096,128]{1,0:T(8,128)(2,1)S(1)}, u32[]{:S(2)}, u32[]{:S(2)}) collective-permute-start(bf16[4096,128]{1,0:T(8,128)(2,1)S(1)} %bitcast.25), channel_id=1, source_target_pairs={{0,16},{16,0},{1,17},{17,1},{2,18},{18,2},{3,19},{19,3},{4,20},{20... | collective-permute-start | bytes 3145736 | tf_op jit(solution)/shard_map/ppermute | solution.py:23
  64.5 2.6 %collective-permute-done.5.s11 = bf16[4096,128]{1,0:T(8,128)(2,1)S(1)} collective-permute-done((bf16[4096,128]{1,0:T(8,128)(2,1)S(1)}, bf16[4096,128]{1,0:T(8,128)(2,1)S(1)}, u32[]{:S(2)}, u32[]{:S(2)}) %collective-permute-start.5) | collective-permute-done | bytes 1048608 | tf_op jit(solution)/shard_map/ppermute | solution.py:23
  67.1 1.0 products.1
  68.1 1.9 %collective-permute-start.9 = (bf16[8,64,128]{2,1,0:T(8,128)(2,1)S(1)}, bf16[8,64,128]{2,1,0:T(8,128)(2,1)S(1)}, u32[]{:S(2)}, u32[]{:S(2)}) collective-permute-start(bf16[8,64,128]{2,1,0:T(8,128)(2,1)S(1)} %get-tuple-element.42.mine), channel_id=1, source_target_pairs={{0,2},{1,3},{2,0},{3,1},{4,6},{5,7},{6,4},{7,5},{8,10},{9,11},{10,... | collective-permute-start | bytes 393224 | tf_op jit(solution)/shard_map/ppermute | solution.py:27
  70.0 1.9 %collective-permute-start.6 = (bf16[8,64,128]{2,1,0:T(8,128)(2,1)S(1)}, bf16[8,64,128]{2,1,0:T(8,128)(2,1)S(1)}, u32[]{:S(2)}, u32[]{:S(2)}) collective-permute-start(bf16[8,64,128]{2,1,0:T(8,128)(2,1)S(1)} %get-tuple-element.38.mine), channel_id=1, source_target_pairs={{0,1},{1,0},{2,3},{3,2},{4,5},{5,4},{6,7},{7,6},{8,9},{9,8},{10,11... | collective-permute-start | bytes 393224 | tf_op jit(solution)/shard_map/ppermute | solution.py:27
  71.9 4.6 %collective-permute-done.9.theirs = bf16[8,64,128]{2,1,0:T(8,128)(2,1)S(1)} collective-permute-done((bf16[8,64,128]{2,1,0:T(8,128)(2,1)S(1)}, bf16[8,64,128]{2,1,0:T(8,128)(2,1)S(1)}, u32[]{:S(2)}, u32[]{:S(2)}) %collective-permute-start.9) | collective-permute-done | bytes 131104 | tf_op jit(solution)/shard_map/ppermute | solution.py:27
  76.5 0.8 collect.3
  77.3 1.9 %collective-permute-start.10 = (bf16[8,64,128]{2,1,0:T(8,128)(2,1)S(1)}, bf16[8,64,128]{2,1,0:T(8,128)(2,1)S(1)}, u32[]{:S(2)}, u32[]{:S(2)}) collective-permute-start(bf16[8,64,128]{2,1,0:T(8,128)(2,1)S(1)} %get-tuple-element.44), channel_id=1, source_target_pairs={{0,1},{1,0},{2,3},{3,2},{4,5},{5,4},{6,7},{7,6},{8,9},{9,8},{10,11... | collective-permute-start | bytes 393224 | tf_op jit(solution)/shard_map/ppermute | solution.py:27
  79.3 0.8 collect.2
  80.1 2.7 %collective-permute-start.7 = (bf16[8,64,128]{2,1,0:T(8,128)(2,1)S(1)}, bf16[8,64,128]{2,1,0:T(8,128)(2,1)S(1)}, u32[]{:S(2)}, u32[]{:S(2)}) collective-permute-start(bf16[8,64,128]{2,1,0:T(8,128)(2,1)S(1)} %get-tuple-element.40), channel_id=1, source_target_pairs={{0,2},{1,3},{2,0},{3,1},{4,6},{5,7},{6,4},{7,5},{8,10},{9,11},{10,... | collective-permute-start | bytes 393224 | tf_op jit(solution)/shard_map/ppermute | solution.py:27
  82.8 1.4 %collective-permute-done.10 = bf16[8,64,128]{2,1,0:T(8,128)(2,1)S(1)} collective-permute-done((bf16[8,64,128]{2,1,0:T(8,128)(2,1)S(1)}, bf16[8,64,128]{2,1,0:T(8,128)(2,1)S(1)}, u32[]{:S(2)}, u32[]{:S(2)}) %collective-permute-start.10) | collective-permute-done | bytes 131104 | tf_op jit(solution)/shard_map/ppermute | solution.py:27
  84.2 5.8 %collective-permute-start.11 = (bf16[4,64,128]{2,1,0:T(8,128)(2,1)S(1)}, bf16[4,64,128]{2,1,0:T(8,128)(2,1)S(1)}, u32[]{:S(2)}, u32[]{:S(2)}) collective-permute-start(bf16[4,64,128]{2,1,0:T(8,128)(2,1)S(1)} %get-tuple-element.46), channel_id=1, source_target_pairs={{0,4},{1,5},{2,6},{3,7},{4,0},{5,1},{6,2},{7,3},{8,12},{9,13},{10,... | collective-permute-start | bytes 196616 | tf_op jit(solution)/shard_map/ppermute | solution.py:27
  90.0 2.4 %collective-permute-done.7 = bf16[8,64,128]{2,1,0:T(8,128)(2,1)S(1)} collective-permute-done((bf16[8,64,128]{2,1,0:T(8,128)(2,1)S(1)}, bf16[8,64,128]{2,1,0:T(8,128)(2,1)S(1)}, u32[]{:S(2)}, u32[]{:S(2)}) %collective-permute-start.7) | collective-permute-done | bytes 131104 | tf_op jit(solution)/shard_map/ppermute | solution.py:27
  92.5 6.2 %collective-permute-start.8 = (bf16[4,64,128]{2,1,0:T(8,128)(2,1)S(1)}, bf16[4,64,128]{2,1,0:T(8,128)(2,1)S(1)}, u32[]{:S(2)}, u32[]{:S(2)}) collective-permute-start(bf16[4,64,128]{2,1,0:T(8,128)(2,1)S(1)} %get-tuple-element.48), channel_id=1, source_target_pairs={{0,4},{1,5},{2,6},{3,7},{4,0},{5,1},{6,2},{7,3},{8,12},{9,13},{10,... | collective-permute-start | bytes 196616 | tf_op jit(solution)/shard_map/ppermute | solution.py:27
  98.8 12.9 %collective-permute-start.13 = (bf16[2,64,128]{2,1,0:T(8,128)(2,1)S(1)}, bf16[2,64,128]{2,1,0:T(8,128)(2,1)S(1)}, u32[]{:S(2)}, u32[]{:S(2)}) collective-permute-start(bf16[2,64,128]{2,1,0:T(8,128)(2,1)S(1)} %get-tuple-element.49), channel_id=1, source_target_pairs={{0,8},{1,9},{2,10},{3,11},{4,12},{5,13},{6,14},{7,15},{8,0},{9,1},... | collective-permute-start | bytes 98312 | tf_op jit(solution)/shard_map/ppermute | solution.py:27
  111.8 5.5 %collective-permute-start.12 = (bf16[2,64,128]{2,1,0:T(8,128)(2,1)S(1)}, bf16[2,64,128]{2,1,0:T(8,128)(2,1)S(1)}, u32[]{:S(2)}, u32[]{:S(2)}) collective-permute-start(bf16[2,64,128]{2,1,0:T(8,128)(2,1)S(1)} %get-tuple-element.51), channel_id=1, source_target_pairs={{0,8},{1,9},{2,10},{3,11},{4,12},{5,13},{6,14},{7,15},{8,0},{9,1},... | collective-permute-start | bytes 98312 | tf_op jit(solution)/shard_map/ppermute | solution.py:27
  117.4 8.9 %collective-permute-done.12.came_first = bf16[2,64,128]{2,1,0:T(8,128)(2,1)S(1)} collective-permute-done((bf16[2,64,128]{2,1,0:T(8,128)(2,1)S(1)}, bf16[2,64,128]{2,1,0:T(8,128)(2,1)S(1)}, u32[]{:S(2)}, u32[]{:S(2)}) %collective-permute-start.12) | collective-permute-done | bytes 32800 | tf_op jit(solution)/shard_map/ppermute | solution.py:27
  126.3 1.3 %finish.1 = bf16[256,128]{1,0:T(8,128)(2,1)} custom-call(s32[16]{0:T(128)S(1)} %pad_add_fusion.anchor, bf16[2,64,128]{2,1,0:T(8,128)(2,1)S(1)} %get-tuple-element.52.first, bf16[2,64,128]{2,1,0:T(8,128)(2,1)S(1)} %get-tuple-element.50.second, bf16[2,64,128]{2,1,0:T(8,128)(2,1)S(1)} %collective-permute-done.12.came_first, ...), custom_call_target="tpu_custom_call" | custom-call | flops 196608 | bytes 327680 | tf_op jit(solution)/shard_map/finish/pallas_call | solution.py:152
  (27 shorter events, 0.3 us)
Async XLA Ops:
  0.0 31.1 %collective-permute-start = (bf16[256,128]{1,0:T(8,128)(2,1)}, bf16[256,128]{1,0:T(8,128)(2,1)S(1)}, u32[]{:S(2)}, u32[]{:S(2)}) collective-permute-start(bf16[256,128]{1,0:T(8,128)(2,1)} %state.1), channel_id=1, source_target_pairs={{512,0},{513,1},{514,2},{515,3},{516,4},{517,5},{518,6},{519,7},{5... | collective-permute-start | bytes 196616 | tf_op jit(solution)/shard_map/ppermute | solution.py:174
  1.3 0.8 copy-start.1
  29.5 7.7 %collective-permute-start.1 = (bf16[256,128]{1,0:T(8,128)(2,1)S(1)}, bf16[256,128]{1,0:T(8,128)(2,1)S(1)}, u32[]{:S(2)}, u32[]{:S(2)}) collective-permute-start(bf16[256,128]{1,0:T(8,128)(2,1)S(1)} %copy-done.1), channel_id=1, source_target_pairs={{0,512},{1,513},{2,514},{3,515},{4,516},{5,517},{6,518},{7,519},{8... | collective-permute-start | bytes 196616 | tf_op jit(solution)/shard_map/ppermute | solution.py:184
  38.4 28.7 %copy-start = (bf16[8,1,128,128]{3,2,1,0:T(8,128)(2,1)S(1)}, bf16[8,1,128,128]{3,2,1,0:T(8,128)(2,1)}, u32[]{:S(2)}) copy-start(bf16[8,1,128,128]{3,2,1,0:T(8,128)(2,1)} %param.11) | copy-start | bytes 786436
  38.4 24.2 %all-to-all-start.2 = ((bf16[16,256,128]{2,1,0:T(8,128)(2,1)}), bf16[16,256,128]{2,1,0:T(8,128)(2,1)S(1)}, u32[]{:S(2)}, u32[]{:S(2)}) async-start(bf16[16,256,128]{2,1,0:T(8,128)(2,1)} %broadcast_in_dim.10), calls=%async_computation.2 | async-start | bytes 2097152 | tf_op jit(solution)/shard_map/all_to_all | solution.py:35
  45.9 0.7 copy-start.2
  45.9 0.7 copy-start.3
  46.7 9.1 %collective-permute-start.2 = (s32[16]{0:T(128)S(1)}, s32[16]{0:T(128)S(1)}, u32[]{:S(2)}, u32[]{:S(2)}) collective-permute-start(s32[16]{0:T(128)S(1)} %pad_add_fusion.1.facts.rows), channel_id=1, source_target_pairs={{0,1},{1,0},{2,3},{3,2},{4,5},{5,4},{6,7},{7,6},{8,9},{9,8},{10,11... | collective-permute-start | bytes 200 | tf_op jit(solution)/shard_map/ppermute | solution.py:27
  48.6 7.2 %collective-permute-start.3 = (s32[16]{0:T(128)S(1)}, s32[16]{0:T(128)S(1)}, u32[]{:S(2)}, u32[]{:S(2)}) collective-permute-start(s32[16]{0:T(128)S(1)} %pad_add_fusion.1.facts.rows), channel_id=1, source_target_pairs={{0,2},{1,3},{2,0},{3,1},{4,6},{5,7},{6,4},{7,5},{8,10},{9,11},{10,... | collective-permute-start | bytes 200 | tf_op jit(solution)/shard_map/ppermute | solution.py:27
  53.8 10.6 %collective-permute-start.4 = (bf16[4096,128]{1,0:T(8,128)(2,1)S(1)}, bf16[4096,128]{1,0:T(8,128)(2,1)S(1)}, u32[]{:S(2)}, u32[]{:S(2)}) collective-permute-start(bf16[4096,128]{1,0:T(8,128)(2,1)S(1)} %bitcast.30), channel_id=1, source_target_pairs={{0,16},{16,0},{1,17},{17,1},{2,18},{18,2},{3,19},{19,3},{4,20},{20... | collective-permute-start | bytes 3145736 | tf_op jit(solution)/shard_map/ppermute | solution.py:23
  62.6 4.5 %collective-permute-start.5 = (bf16[4096,128]{1,0:T(8,128)(2,1)S(1)}, bf16[4096,128]{1,0:T(8,128)(2,1)S(1)}, u32[]{:S(2)}, u32[]{:S(2)}) collective-permute-start(bf16[4096,128]{1,0:T(8,128)(2,1)S(1)} %bitcast.25), channel_id=1, source_target_pairs={{0,16},{16,0},{1,17},{17,1},{2,18},{18,2},{3,19},{19,3},{4,20},{20... | collective-permute-start | bytes 3145736 | tf_op jit(solution)/shard_map/ppermute | solution.py:23
  68.1 8.4 %collective-permute-start.9 = (bf16[8,64,128]{2,1,0:T(8,128)(2,1)S(1)}, bf16[8,64,128]{2,1,0:T(8,128)(2,1)S(1)}, u32[]{:S(2)}, u32[]{:S(2)}) collective-permute-start(bf16[8,64,128]{2,1,0:T(8,128)(2,1)S(1)} %get-tuple-element.42.mine), channel_id=1, source_target_pairs={{0,2},{1,3},{2,0},{3,1},{4,6},{5,7},{6,4},{7,5},{8,10},{9,11},{10,... | collective-permute-start | bytes 393224 | tf_op jit(solution)/shard_map/ppermute | solution.py:27
  70.0 9.2 %collective-permute-start.6 = (bf16[8,64,128]{2,1,0:T(8,128)(2,1)S(1)}, bf16[8,64,128]{2,1,0:T(8,128)(2,1)S(1)}, u32[]{:S(2)}, u32[]{:S(2)}) collective-permute-start(bf16[8,64,128]{2,1,0:T(8,128)(2,1)S(1)} %get-tuple-element.38.mine), channel_id=1, source_target_pairs={{0,1},{1,0},{2,3},{3,2},{4,5},{5,4},{6,7},{7,6},{8,9},{9,8},{10,11... | collective-permute-start | bytes 393224 | tf_op jit(solution)/shard_map/ppermute | solution.py:27
  77.3 6.9 %collective-permute-start.10 = (bf16[8,64,128]{2,1,0:T(8,128)(2,1)S(1)}, bf16[8,64,128]{2,1,0:T(8,128)(2,1)S(1)}, u32[]{:S(2)}, u32[]{:S(2)}) collective-permute-start(bf16[8,64,128]{2,1,0:T(8,128)(2,1)S(1)} %get-tuple-element.44), channel_id=1, source_target_pairs={{0,1},{1,0},{2,3},{3,2},{4,5},{5,4},{6,7},{7,6},{8,9},{9,8},{10,11... | collective-permute-start | bytes 393224 | tf_op jit(solution)/shard_map/ppermute | solution.py:27
  80.1 12.4 %collective-permute-start.7 = (bf16[8,64,128]{2,1,0:T(8,128)(2,1)S(1)}, bf16[8,64,128]{2,1,0:T(8,128)(2,1)S(1)}, u32[]{:S(2)}, u32[]{:S(2)}) collective-permute-start(bf16[8,64,128]{2,1,0:T(8,128)(2,1)S(1)} %get-tuple-element.40), channel_id=1, source_target_pairs={{0,2},{1,3},{2,0},{3,1},{4,6},{5,7},{6,4},{7,5},{8,10},{9,11},{10,... | collective-permute-start | bytes 393224 | tf_op jit(solution)/shard_map/ppermute | solution.py:27
  84.2 14.5 %collective-permute-start.11 = (bf16[4,64,128]{2,1,0:T(8,128)(2,1)S(1)}, bf16[4,64,128]{2,1,0:T(8,128)(2,1)S(1)}, u32[]{:S(2)}, u32[]{:S(2)}) collective-permute-start(bf16[4,64,128]{2,1,0:T(8,128)(2,1)S(1)} %get-tuple-element.46), channel_id=1, source_target_pairs={{0,4},{1,5},{2,6},{3,7},{4,0},{5,1},{6,2},{7,3},{8,12},{9,13},{10,... | collective-permute-start | bytes 196616 | tf_op jit(solution)/shard_map/ppermute | solution.py:27
  92.5 19.2 %collective-permute-start.8 = (bf16[4,64,128]{2,1,0:T(8,128)(2,1)S(1)}, bf16[4,64,128]{2,1,0:T(8,128)(2,1)S(1)}, u32[]{:S(2)}, u32[]{:S(2)}) collective-permute-start(bf16[4,64,128]{2,1,0:T(8,128)(2,1)S(1)} %get-tuple-element.48), channel_id=1, source_target_pairs={{0,4},{1,5},{2,6},{3,7},{4,0},{5,1},{6,2},{7,3},{8,12},{9,13},{10,... | collective-permute-start | bytes 196616 | tf_op jit(solution)/shard_map/ppermute | solution.py:27
  98.8 18.6 %collective-permute-start.13 = (bf16[2,64,128]{2,1,0:T(8,128)(2,1)S(1)}, bf16[2,64,128]{2,1,0:T(8,128)(2,1)S(1)}, u32[]{:S(2)}, u32[]{:S(2)}) collective-permute-start(bf16[2,64,128]{2,1,0:T(8,128)(2,1)S(1)} %get-tuple-element.49), channel_id=1, source_target_pairs={{0,8},{1,9},{2,10},{3,11},{4,12},{5,13},{6,14},{7,15},{8,0},{9,1},... | collective-permute-start | bytes 98312 | tf_op jit(solution)/shard_map/ppermute | solution.py:27
  111.7 5.6 %copy-start.4 = (s32[8]{0:T(128)S(1)}, s32[8]{0:T(128)}, u32[]{:S(2)}) copy-start(s32[8]{0:T(128)} %param.15) | copy-start | bytes 100
  111.7 5.6 %copy-start.5 = (s32[8]{0:T(128)S(1)}, s32[8]{0:T(128)}, u32[]{:S(2)}) copy-start(s32[8]{0:T(128)} %param.14) | copy-start | bytes 100
  111.8 14.5 %collective-permute-start.12 = (bf16[2,64,128]{2,1,0:T(8,128)(2,1)S(1)}, bf16[2,64,128]{2,1,0:T(8,128)(2,1)S(1)}, u32[]{:S(2)}, u32[]{:S(2)}) collective-permute-start(bf16[2,64,128]{2,1,0:T(8,128)(2,1)S(1)} %get-tuple-element.51), channel_id=1, source_target_pairs={{0,8},{1,9},{2,10},{3,11},{4,12},{5,13},{6,14},{7,15},{8,0},{9,1},... | collective-permute-start | bytes 98312 | tf_op jit(solution)/shard_map/ppermute | solution.py:27

commit v5 on v4

--- a/solution.py
+++ b/solution.py
@@ -10,6 +10,7 @@
 WIDE = ("zh", "x", "y", "c")
 PLANE = ("x", "y")
 HALF, SIDE, LINE = 2, 4, 16
+FIRST = 3
 N_PLANE = SIDE * SIDE
 SMEM = pl.BlockSpec(memory_space=pltpu.SMEM)
 VMEM = pl.BlockSpec(memory_space=pltpu.VMEM)
@@ -55,7 +56,7 @@
 
 def product_kernel(facts, values, s00, s01, s10, s11, first, second, picked):
     count, width = values.shape[:2]
-    half = width // 2
+    cut = first.shape[1]
     shift = (s00.shape[0] // width // N_PLANE).bit_length() - 1
     zh, mine = lax.axis_index("zh"), lax.axis_index("c")
     for k in range(count):
@@ -72,17 +73,18 @@
 
     for k in range(count):
         out = jnp.dot(values[k], picked[k], preferred_element_type=jnp.float32)
-        first[k] = out[:half].astype(first.dtype)
-        second[k] = out[half:].astype(second.dtype)
+        first[k] = out[:cut].astype(first.dtype)
+        second[k] = out[cut:].astype(second.dtype)
 
 
 def products(facts, values, sources):
     count, width, _ = values.shape
     labels = sources[0].shape[-1]
-    part = jax.ShapeDtypeStruct((count, width // 2, labels), jnp.bfloat16)
+    cut = width * FIRST // 8
+    parts = [(count, rows, labels) for rows in (cut, width - cut)]
     return pl.pallas_call(
         product_kernel,
-        out_shape=(part, part),
+        out_shape=[jax.ShapeDtypeStruct(part, jnp.bfloat16) for part in parts],
         in_specs=[SMEM] + [VMEM] * 5,
         out_specs=(VMEM, VMEM),
         scratch_shapes=[pltpu.VMEM((count, width, labels), jnp.bfloat16)],
@@ -131,11 +133,12 @@
 
 def finish_kernel(anchor, first, second, came_first, came_second, state, out, result):
     docs, labels = state.shape
-    slots, half = first.shape[:2]
+    slots, cut = first.shape[:2]
+    width = docs // slots
     lane = lax.broadcasted_iota(jnp.int32, (1, labels), 1)
     for slot in range(slots):
         for side, (keep, came) in enumerate(((first, came_first), (second, came_second))):
-            here = pl.ds((slot * 2 + side) * half, half)
+            here = pl.ds(slot * width + side * cut, keep.shape[1])
             total = keep[slot].astype(jnp.float32) + came[slot].astype(jnp.float32)
             total = total + state[here].astype(jnp.float32)
             result[here] = total / jnp.sum(total, axis=-1, keepdims=True)

time: 128 us -> 131 us (1.023)
  the two profiles are of different devices: /device:TPU:8 before, /device:TPU:26 now
where the time goes in v5:
time: 131 us; the launch traced here: 130 us
  starting transfers between devices  66.5 us (51%)
  waiting for transfers between devices  31.9 us (24%)
  blocking collectives  24.5 us (19%)
  Pallas kernels  3.89 us (3%)
  local copies, waits for them, and re-layouts  2.87 us (2%)
    ppermute x10, starting transfers between devices, exchange(): return lax.ppermute(value, 'zl', [(i, i ^ step) for i in range(LINE)])  49.8 us
    all_to_all x1, blocking collectives, plane_exchange(): return lax.all_to_all(value, PLANE, 0, 0)  24.5 us
    ppermute x10, waiting for transfers between devices, exchange(): return lax.ppermute(value, 'zl', [(i, i ^ step) for i in range(LINE)])  19.2 us
    all_to_all x1, starting transfers between devices, plane_exchange(): return lax.all_to_all(value, PLANE, 0, 0)  7.27 us
    ppermute x1, waiting for transfers between devices, local(): from_first = lax.ppermute(again, 'zh', [(0, 1)])  6.06 us
    ppermute x1, starting transfers between devices, local(): from_first = lax.ppermute(again, 'zh', [(0, 1)])  4.31 us
    all_to_all x1, waiting for transfers between devices, plane_exchange(): return lax.all_to_all(value, PLANE, 0, 0)  4.04 us
    ppermute x2, starting transfers between devices, swap(): return lax.ppermute(value, axis, [(0, 1), (1, 0)])  3.83 us
  transfers between devices with their start and end apart: 15, of which 7 were waited for; matrix products, arithmetic and copies ran while one was open for 0% of the time, Pallas kernels for 1%

profile of v5, /device:TPU:26, one launch (start us, length us, event | category | flops | bytes accessed | tf_op | source)
XLA Modules:
  0.0 130.1 jit_solution(12000098108778306967)
XLA Ops:
  0.0 1.3 collective-permute-start
  1.3 0.8 copy-done.1
  2.1 24.7 %conditional.2 = (bf16[16,256,128]{2,1,0:T(8,128)(2,1)S(1)}) conditional(s32[]{:T(128)} %convert_element_type.7, bf16[16,256,128]{2,1,0:T(8,128)(2,1)S(1)} %blank.1, bf16[256,128]{1,0:T(8,128)(2,1)S(1)} %copy-done.1), branch_computations={%region_0.0_spmd, %region_1.0_spmd} | conditional | bytes 3211272 | solution.py:183
  2.1 0.2 broadcast_in_dim.2
  2.3 24.5 %all_to_all.13 = bf16[16,256,128]{2,1,0:T(8,128)(2,1)S(1)} all-to-all(bf16[16,256,128]{2,1,0:T(8,128)(2,1)S(1)} %broadcast_in_dim.2), channel_id=1, replica_groups=mesh['zh'=2,'x'=4,'y'=4,'c'=2,'zl'=16] {'x','y'}, dimensions={0} | all-to-all | bytes 2097152 | tf_op jit(solution)/shard_map/cond/branch_1_fun/all_to_all | solution.py:36
  26.8 4.3 %collective-permute-start.1 = (bf16[256,128]{1,0:T(8,128)(2,1)S(1)}, bf16[256,128]{1,0:T(8,128)(2,1)S(1)}, u32[]{:S(2)}, u32[]{:S(2)}) collective-permute-start(bf16[256,128]{1,0:T(8,128)(2,1)S(1)} %copy-done.1), channel_id=1, source_target_pairs={{0,512},{1,513},{2,514},{3,515},{4,516},{5,517},{6,518},{7,519},{8... | collective-permute-start | bytes 196616 | tf_op jit(solution)/shard_map/ppermute | solution.py:187
  31.1 6.1 %collective-permute-done.1 = bf16[256,128]{1,0:T(8,128)(2,1)S(1)} collective-permute-done((bf16[256,128]{1,0:T(8,128)(2,1)S(1)}, bf16[256,128]{1,0:T(8,128)(2,1)S(1)}, u32[]{:S(2)}, u32[]{:S(2)}) %collective-permute-start.1) | collective-permute-done | bytes 65568 | tf_op jit(solution)/shard_map/ppermute | solution.py:187
  37.2 1.2 broadcast_in_dim.10
  38.4 7.3 %all-to-all-start.2 = ((bf16[16,256,128]{2,1,0:T(8,128)(2,1)}), bf16[16,256,128]{2,1,0:T(8,128)(2,1)S(1)}, u32[]{:S(2)}, u32[]{:S(2)}) async-start(bf16[16,256,128]{2,1,0:T(8,128)(2,1)} %broadcast_in_dim.10), calls=%async_computation.2 | async-start | bytes 2097152 | tf_op jit(solution)/shard_map/all_to_all | solution.py:36
  45.7 0.6 copy-done.2
  46.4 1.9 %collective-permute-start.2 = (s32[16]{0:T(128)S(1)}, s32[16]{0:T(128)S(1)}, u32[]{:S(2)}, u32[]{:S(2)}) collective-permute-start(s32[16]{0:T(128)S(1)} %pad_add_fusion.1.facts.rows), channel_id=1, source_target_pairs={{0,1},{1,0},{2,3},{3,2},{4,5},{5,4},{6,7},{7,6},{8,9},{9,8},{10,11... | collective-permute-start | bytes 200 | tf_op jit(solution)/shard_map/ppermute | solution.py:28
  48.3 5.2 %collective-permute-start.3 = (s32[16]{0:T(128)S(1)}, s32[16]{0:T(128)S(1)}, u32[]{:S(2)}, u32[]{:S(2)}) collective-permute-start(s32[16]{0:T(128)S(1)} %pad_add_fusion.1.facts.rows), channel_id=1, source_target_pairs={{0,2},{1,3},{2,0},{3,1},{4,6},{5,7},{6,4},{7,5},{8,10},{9,11},{10,... | collective-permute-start | bytes 200 | tf_op jit(solution)/shard_map/ppermute | solution.py:28
  53.6 1.9 %collective-permute-start.4 = (bf16[4096,128]{1,0:T(8,128)(2,1)S(1)}, bf16[4096,128]{1,0:T(8,128)(2,1)S(1)}, u32[]{:S(2)}, u32[]{:S(2)}) collective-permute-start(bf16[4096,128]{1,0:T(8,128)(2,1)S(1)} %bitcast.30), channel_id=1, source_target_pairs={{0,16},{16,0},{1,17},{17,1},{2,18},{18,2},{3,19},{19,3},{4,20},{20... | collective-permute-start | bytes 3145736 | tf_op jit(solution)/shard_map/ppermute | solution.py:24
  55.5 4.0 %all-to-all-done.2 = bf16[16,256,128]{2,1,0:T(8,128)(2,1)S(1)} async-done(((bf16[16,256,128]{2,1,0:T(8,128)(2,1)}), bf16[16,256,128]{2,1,0:T(8,128)(2,1)S(1)}, u32[]{:S(2)}, u32[]{:S(2)}) %all-to-all-start.2) | async-done | bytes 1048608 | tf_op jit(solution)/shard_map/all_to_all | solution.py:36
  59.6 1.9 %collective-permute-start.5 = (bf16[4096,128]{1,0:T(8,128)(2,1)S(1)}, bf16[4096,128]{1,0:T(8,128)(2,1)S(1)}, u32[]{:S(2)}, u32[]{:S(2)}) collective-permute-start(bf16[4096,128]{1,0:T(8,128)(2,1)S(1)} %bitcast.25), channel_id=1, source_target_pairs={{0,16},{16,0},{1,17},{17,1},{2,18},{18,2},{3,19},{19,3},{4,20},{20... | collective-permute-start | bytes 3145736 | tf_op jit(solution)/shard_map/ppermute | solution.py:24
  61.5 2.6 %collective-permute-done.5.s11 = bf16[4096,128]{1,0:T(8,128)(2,1)S(1)} collective-permute-done((bf16[4096,128]{1,0:T(8,128)(2,1)S(1)}, bf16[4096,128]{1,0:T(8,128)(2,1)S(1)}, u32[]{:S(2)}, u32[]{:S(2)}) %collective-permute-start.5) | collective-permute-done | bytes 1048608 | tf_op jit(solution)/shard_map/ppermute | solution.py:24
  64.1 1.0 products.1
  65.1 1.9 %collective-permute-start.9 = (bf16[8,80,128]{2,1,0:T(8,128)(2,1)S(1)}, bf16[8,80,128]{2,1,0:T(8,128)(2,1)S(1)}, u32[]{:S(2)}, u32[]{:S(2)}) collective-permute-start(bf16[8,80,128]{2,1,0:T(8,128)(2,1)S(1)} %get-tuple-element.42.mine), channel_id=1, source_target_pairs={{0,2},{1,3},{2,0},{3,1},{4,6},{5,7},{6,4},{7,5},{8,10},{9,11},{10,... | collective-permute-start | bytes 491528 | tf_op jit(solution)/shard_map/ppermute | solution.py:28
  67.0 2.3 %collective-permute-start.6 = (bf16[8,48,128]{2,1,0:T(8,128)(2,1)S(1)}, bf16[8,48,128]{2,1,0:T(8,128)(2,1)S(1)}, u32[]{:S(2)}, u32[]{:S(2)}) collective-permute-start(bf16[8,48,128]{2,1,0:T(8,128)(2,1)S(1)} %get-tuple-element.38.mine), channel_id=1, source_target_pairs={{0,1},{1,0},{2,3},{3,2},{4,5},{5,4},{6,7},{7,6},{8,9},{9,8},{10,11... | collective-permute-start | bytes 294920 | tf_op jit(solution)/shard_map/ppermute | solution.py:28
  69.4 7.8 %collective-permute-done.6.theirs = bf16[8,48,128]{2,1,0:T(8,128)(2,1)S(1)} collective-permute-done((bf16[8,48,128]{2,1,0:T(8,128)(2,1)S(1)}, bf16[8,48,128]{2,1,0:T(8,128)(2,1)S(1)}, u32[]{:S(2)}, u32[]{:S(2)}) %collective-permute-start.6) | collective-permute-done | bytes 98336 | tf_op jit(solution)/shard_map/ppermute | solution.py:28
  77.2 0.8 collect.2
  78.0 1.9 %collective-permute-start.7 = (bf16[8,48,128]{2,1,0:T(8,128)(2,1)S(1)}, bf16[8,48,128]{2,1,0:T(8,128)(2,1)S(1)}, u32[]{:S(2)}, u32[]{:S(2)}) collective-permute-start(bf16[8,48,128]{2,1,0:T(8,128)(2,1)S(1)} %get-tuple-element.40), channel_id=1, source_target_pairs={{0,2},{1,3},{2,0},{3,1},{4,6},{5,7},{6,4},{7,5},{8,10},{9,11},{10,... | collective-permute-start | bytes 294920 | tf_op jit(solution)/shard_map/ppermute | solution.py:28
  79.9 0.8 collect.3
  80.7 3.5 %collective-permute-start.10 = (bf16[8,80,128]{2,1,0:T(8,128)(2,1)S(1)}, bf16[8,80,128]{2,1,0:T(8,128)(2,1)S(1)}, u32[]{:S(2)}, u32[]{:S(2)}) collective-permute-start(bf16[8,80,128]{2,1,0:T(8,128)(2,1)S(1)} %get-tuple-element.44), channel_id=1, source_target_pairs={{0,1},{1,0},{2,3},{3,2},{4,5},{5,4},{6,7},{7,6},{8,9},{9,8},{10,11... | collective-permute-start | bytes 491528 | tf_op jit(solution)/shard_map/ppermute | solution.py:28
  84.3 2.1 %collective-permute-done.7 = bf16[8,48,128]{2,1,0:T(8,128)(2,1)S(1)} collective-permute-done((bf16[8,48,128]{2,1,0:T(8,128)(2,1)S(1)}, bf16[8,48,128]{2,1,0:T(8,128)(2,1)S(1)}, u32[]{:S(2)}, u32[]{:S(2)}) %collective-permute-start.7) | collective-permute-done | bytes 98336 | tf_op jit(solution)/shard_map/ppermute | solution.py:28
  86.3 5.9 %collective-permute-start.8 = (bf16[4,48,128]{2,1,0:T(8,128)(2,1)S(1)}, bf16[4,48,128]{2,1,0:T(8,128)(2,1)S(1)}, u32[]{:S(2)}, u32[]{:S(2)}) collective-permute-start(bf16[4,48,128]{2,1,0:T(8,128)(2,1)S(1)} %get-tuple-element.48), channel_id=1, source_target_pairs={{0,4},{1,5},{2,6},{3,7},{4,0},{5,1},{6,2},{7,3},{8,12},{9,13},{10,... | collective-permute-start | bytes 147464 | tf_op jit(solution)/shard_map/ppermute | solution.py:28
  92.3 3.9 %collective-permute-start.11 = (bf16[4,80,128]{2,1,0:T(8,128)(2,1)S(1)}, bf16[4,80,128]{2,1,0:T(8,128)(2,1)S(1)}, u32[]{:S(2)}, u32[]{:S(2)}) collective-permute-start(bf16[4,80,128]{2,1,0:T(8,128)(2,1)S(1)} %get-tuple-element.46), channel_id=1, source_target_pairs={{0,4},{1,5},{2,6},{3,7},{4,0},{5,1},{6,2},{7,3},{8,12},{9,13},{10,... | collective-permute-start | bytes 245768 | tf_op jit(solution)/shard_map/ppermute | solution.py:28
  96.2 1.2 collective-permute-done.8
  97.4 14.3 %collective-permute-start.12 = (bf16[2,48,128]{2,1,0:T(8,128)(2,1)S(1)}, bf16[2,48,128]{2,1,0:T(8,128)(2,1)S(1)}, u32[]{:S(2)}, u32[]{:S(2)}) collective-permute-start(bf16[2,48,128]{2,1,0:T(8,128)(2,1)S(1)} %get-tuple-element.51), channel_id=1, source_target_pairs={{0,8},{1,9},{2,10},{3,11},{4,12},{5,13},{6,14},{7,15},{8,0},{9,1},... | collective-permute-start | bytes 73736 | tf_op jit(solution)/shard_map/ppermute | solution.py:28
  111.7 8.9 %collective-permute-start.13 = (bf16[2,80,128]{2,1,0:T(8,128)(2,1)S(1)}, bf16[2,80,128]{2,1,0:T(8,128)(2,1)S(1)}, u32[]{:S(2)}, u32[]{:S(2)}) collective-permute-start(bf16[2,80,128]{2,1,0:T(8,128)(2,1)S(1)} %get-tuple-element.49), channel_id=1, source_target_pairs={{0,8},{1,9},{2,10},{3,11},{4,12},{5,13},{6,14},{7,15},{8,0},{9,1},... | collective-permute-start | bytes 122888 | tf_op jit(solution)/shard_map/ppermute | solution.py:28
  120.7 8.1 %collective-permute-done.13.came_second = bf16[2,80,128]{2,1,0:T(8,128)(2,1)S(1)} collective-permute-done((bf16[2,80,128]{2,1,0:T(8,128)(2,1)S(1)}, bf16[2,80,128]{2,1,0:T(8,128)(2,1)S(1)}, u32[]{:S(2)}, u32[]{:S(2)}) %collective-permute-start.13) | collective-permute-done | bytes 40992 | tf_op jit(solution)/shard_map/ppermute | solution.py:28
  128.8 1.3 %finish.1 = bf16[256,128]{1,0:T(8,128)(2,1)} custom-call(s32[16]{0:T(128)S(1)} %pad_add_fusion.anchor, bf16[2,48,128]{2,1,0:T(8,128)(2,1)S(1)} %get-tuple-element.52.first, bf16[2,80,128]{2,1,0:T(8,128)(2,1)S(1)} %get-tuple-element.50.second, bf16[2,48,128]{2,1,0:T(8,128)(2,1)S(1)} %collective-permute-done.12.came_first, ...), custom_call_target="tpu_custom_call" | custom-call | flops 196608 | bytes 327680 | tf_op jit(solution)/shard_map/finish/pallas_call | solution.py:155
  (27 shorter events, 0.3 us)
Async XLA Ops:
  0.0 31.1 %collective-permute-start = (bf16[256,128]{1,0:T(8,128)(2,1)}, bf16[256,128]{1,0:T(8,128)(2,1)S(1)}, u32[]{:S(2)}, u32[]{:S(2)}) collective-permute-start(bf16[256,128]{1,0:T(8,128)(2,1)} %state.1), channel_id=1, source_target_pairs={{512,0},{513,1},{514,2},{515,3},{516,4},{517,5},{518,6},{519,7},{5... | collective-permute-start | bytes 196616 | tf_op jit(solution)/shard_map/ppermute | solution.py:177
  1.3 0.8 copy-start.1
  26.8 10.4 %collective-permute-start.1 = (bf16[256,128]{1,0:T(8,128)(2,1)S(1)}, bf16[256,128]{1,0:T(8,128)(2,1)S(1)}, u32[]{:S(2)}, u32[]{:S(2)}) collective-permute-start(bf16[256,128]{1,0:T(8,128)(2,1)S(1)} %copy-done.1), channel_id=1, source_target_pairs={{0,512},{1,513},{2,514},{3,515},{4,516},{5,517},{6,518},{7,519},{8... | collective-permute-start | bytes 196616 | tf_op jit(solution)/shard_map/ppermute | solution.py:187
  38.4 25.7 %copy-start = (bf16[8,1,128,128]{3,2,1,0:T(8,128)(2,1)S(1)}, bf16[8,1,128,128]{3,2,1,0:T(8,128)(2,1)}, u32[]{:S(2)}) copy-start(bf16[8,1,128,128]{3,2,1,0:T(8,128)(2,1)} %param.11) | copy-start | bytes 786436
  38.4 21.2 %all-to-all-start.2 = ((bf16[16,256,128]{2,1,0:T(8,128)(2,1)}), bf16[16,256,128]{2,1,0:T(8,128)(2,1)S(1)}, u32[]{:S(2)}, u32[]{:S(2)}) async-start(bf16[16,256,128]{2,1,0:T(8,128)(2,1)} %broadcast_in_dim.10), calls=%async_computation.2 | async-start | bytes 2097152 | tf_op jit(solution)/shard_map/all_to_all | solution.py:36
  45.7 0.7 copy-start.2
  45.7 0.7 copy-start.3
  46.4 9.1 %collective-permute-start.2 = (s32[16]{0:T(128)S(1)}, s32[16]{0:T(128)S(1)}, u32[]{:S(2)}, u32[]{:S(2)}) collective-permute-start(s32[16]{0:T(128)S(1)} %pad_add_fusion.1.facts.rows), channel_id=1, source_target_pairs={{0,1},{1,0},{2,3},{3,2},{4,5},{5,4},{6,7},{7,6},{8,9},{9,8},{10,11... | collective-permute-start | bytes 200 | tf_op jit(solution)/shard_map/ppermute | solution.py:28
  48.3 7.2 %collective-permute-start.3 = (s32[16]{0:T(128)S(1)}, s32[16]{0:T(128)S(1)}, u32[]{:S(2)}, u32[]{:S(2)}) collective-permute-start(s32[16]{0:T(128)S(1)} %pad_add_fusion.1.facts.rows), channel_id=1, source_target_pairs={{0,2},{1,3},{2,0},{3,1},{4,6},{5,7},{6,4},{7,5},{8,10},{9,11},{10,... | collective-permute-start | bytes 200 | tf_op jit(solution)/shard_map/ppermute | solution.py:28
  53.6 7.9 %collective-permute-start.4 = (bf16[4096,128]{1,0:T(8,128)(2,1)S(1)}, bf16[4096,128]{1,0:T(8,128)(2,1)S(1)}, u32[]{:S(2)}, u32[]{:S(2)}) collective-permute-start(bf16[4096,128]{1,0:T(8,128)(2,1)S(1)} %bitcast.30), channel_id=1, source_target_pairs={{0,16},{16,0},{1,17},{17,1},{2,18},{18,2},{3,19},{19,3},{4,20},{20... | collective-permute-start | bytes 3145736 | tf_op jit(solution)/shard_map/ppermute | solution.py:24
  59.6 4.5 %collective-permute-start.5 = (bf16[4096,128]{1,0:T(8,128)(2,1)S(1)}, bf16[4096,128]{1,0:T(8,128)(2,1)S(1)}, u32[]{:S(2)}, u32[]{:S(2)}) collective-permute-start(bf16[4096,128]{1,0:T(8,128)(2,1)S(1)} %bitcast.25), channel_id=1, source_target_pairs={{0,16},{16,0},{1,17},{17,1},{2,18},{18,2},{3,19},{19,3},{4,20},{20... | collective-permute-start | bytes 3145736 | tf_op jit(solution)/shard_map/ppermute | solution.py:24
  65.1 14.8 %collective-permute-start.9 = (bf16[8,80,128]{2,1,0:T(8,128)(2,1)S(1)}, bf16[8,80,128]{2,1,0:T(8,128)(2,1)S(1)}, u32[]{:S(2)}, u32[]{:S(2)}) collective-permute-start(bf16[8,80,128]{2,1,0:T(8,128)(2,1)S(1)} %get-tuple-element.42.mine), channel_id=1, source_target_pairs={{0,2},{1,3},{2,0},{3,1},{4,6},{5,7},{6,4},{7,5},{8,10},{9,11},{10,... | collective-permute-start | bytes 491528 | tf_op jit(solution)/shard_map/ppermute | solution.py:28
  67.0 10.1 %collective-permute-start.6 = (bf16[8,48,128]{2,1,0:T(8,128)(2,1)S(1)}, bf16[8,48,128]{2,1,0:T(8,128)(2,1)S(1)}, u32[]{:S(2)}, u32[]{:S(2)}) collective-permute-start(bf16[8,48,128]{2,1,0:T(8,128)(2,1)S(1)} %get-tuple-element.38.mine), channel_id=1, source_target_pairs={{0,1},{1,0},{2,3},{3,2},{4,5},{5,4},{6,7},{7,6},{8,9},{9,8},{10,11... | collective-permute-start | bytes 294920 | tf_op jit(solution)/shard_map/ppermute | solution.py:28
  78.0 8.3 %collective-permute-start.7 = (bf16[8,48,128]{2,1,0:T(8,128)(2,1)S(1)}, bf16[8,48,128]{2,1,0:T(8,128)(2,1)S(1)}, u32[]{:S(2)}, u32[]{:S(2)}) collective-permute-start(bf16[8,48,128]{2,1,0:T(8,128)(2,1)S(1)} %get-tuple-element.40), channel_id=1, source_target_pairs={{0,2},{1,3},{2,0},{3,1},{4,6},{5,7},{6,4},{7,5},{8,10},{9,11},{10,... | collective-permute-start | bytes 294920 | tf_op jit(solution)/shard_map/ppermute | solution.py:28
  80.7 11.5 %collective-permute-start.10 = (bf16[8,80,128]{2,1,0:T(8,128)(2,1)S(1)}, bf16[8,80,128]{2,1,0:T(8,128)(2,1)S(1)}, u32[]{:S(2)}, u32[]{:S(2)}) collective-permute-start(bf16[8,80,128]{2,1,0:T(8,128)(2,1)S(1)} %get-tuple-element.44), channel_id=1, source_target_pairs={{0,1},{1,0},{2,3},{3,2},{4,5},{5,4},{6,7},{7,6},{8,9},{9,8},{10,11... | collective-permute-start | bytes 491528 | tf_op jit(solution)/shard_map/ppermute | solution.py:28
  86.3 11.0 %collective-permute-start.8 = (bf16[4,48,128]{2,1,0:T(8,128)(2,1)S(1)}, bf16[4,48,128]{2,1,0:T(8,128)(2,1)S(1)}, u32[]{:S(2)}, u32[]{:S(2)}) collective-permute-start(bf16[4,48,128]{2,1,0:T(8,128)(2,1)S(1)} %get-tuple-element.48), channel_id=1, source_target_pairs={{0,4},{1,5},{2,6},{3,7},{4,0},{5,1},{6,2},{7,3},{8,12},{9,13},{10,... | collective-permute-start | bytes 147464 | tf_op jit(solution)/shard_map/ppermute | solution.py:28
  92.3 19.4 %collective-permute-start.11 = (bf16[4,80,128]{2,1,0:T(8,128)(2,1)S(1)}, bf16[4,80,128]{2,1,0:T(8,128)(2,1)S(1)}, u32[]{:S(2)}, u32[]{:S(2)}) collective-permute-start(bf16[4,80,128]{2,1,0:T(8,128)(2,1)S(1)} %get-tuple-element.46), channel_id=1, source_target_pairs={{0,4},{1,5},{2,6},{3,7},{4,0},{5,1},{6,2},{7,3},{8,12},{9,13},{10,... | collective-permute-start | bytes 245768 | tf_op jit(solution)/shard_map/ppermute | solution.py:28
  97.4 23.4 %collective-permute-start.12 = (bf16[2,48,128]{2,1,0:T(8,128)(2,1)S(1)}, bf16[2,48,128]{2,1,0:T(8,128)(2,1)S(1)}, u32[]{:S(2)}, u32[]{:S(2)}) collective-permute-start(bf16[2,48,128]{2,1,0:T(8,128)(2,1)S(1)} %get-tuple-element.51), channel_id=1, source_target_pairs={{0,8},{1,9},{2,10},{3,11},{4,12},{5,13},{6,14},{7,15},{8,0},{9,1},... | collective-permute-start | bytes 73736 | tf_op jit(solution)/shard_map/ppermute | solution.py:28
  111.7 8.9 %copy-start.4 = (s32[8]{0:T(128)S(1)}, s32[8]{0:T(128)}, u32[]{:S(2)}) copy-start(s32[8]{0:T(128)} %param.15) | copy-start | bytes 100
  111.7 8.9 %copy-start.5 = (s32[8]{0:T(128)S(1)}, s32[8]{0:T(128)}, u32[]{:S(2)}) copy-start(s32[8]{0:T(128)} %param.14) | copy-start | bytes 100
  111.7 17.1 %collective-permute-start.13 = (bf16[2,80,128]{2,1,0:T(8,128)(2,1)S(1)}, bf16[2,80,128]{2,1,0:T(8,128)(2,1)S(1)}, u32[]{:S(2)}, u32[]{:S(2)}) collective-permute-start(bf16[2,80,128]{2,1,0:T(8,128)(2,1)S(1)} %get-tuple-element.49), channel_id=1, source_target_pairs={{0,8},{1,9},{2,10},{3,11},{4,12},{5,13},{6,14},{7,15},{8,0},{9,1},... | collective-permute-start | bytes 122888 | tf_op jit(solution)/shard_map/ppermute | solution.py:28
